TPU v7x, 128 devices: a whole 4x4x4 slice. The times are simulated.
128 devices in a mesh: owner: 16 (over z, y), group: 8 (over x, core).
Axes of the slice: x: 4, y: 4, z: 4, core: 2. Of those that a mesh axis runs over, the one named last changes fastest.
Arguments:
- memory: bfloat16 [262144, 512], P(('owner', 'group')), may hold values from -64 to 64
- touched: int32 [128, 128, 4], P(('owner', 'group')), may hold values from 0 to 2047
- src_pos: int32 [65536], P(('owner', 'group')), may hold values from 0 to 511
- dst_owner: int32 [65536, 1], P(('owner', 'group')), may hold values from 0 to 127; in each aligned block of 512 rows (0 to 511, 512 to 1023, ...) at most 8 rows name the same one
- dst_slot: int32 [65536], P(('owner', 'group')), may hold values from 0 to 3
- neighbors: int32 [65536, 16], P(('owner', 'group')), may hold values from 0 to 511
- ev_time: int32 [65536], P(('owner', 'group')), may hold values from 0 to 4095
- neigh_time: int32 [65536, 16], P(('owner', 'group')), may hold values from 0 to 4095
- time_freq: float32 [128], replicated, may hold values from 0.001 to 0.5
- w_query: bfloat16 [512, 512], replicated, may hold values from -0.25 to 0.25
- w_key: bfloat16 [640, 512], replicated, may hold values from -0.25 to 0.25
- w_value: bfloat16 [640, 512], replicated, may hold values from -0.25 to 0.25
- w_out: bfloat16 [512, 512], replicated, may hold values from -0.25 to 0.25
- w_msg1: bfloat16 [1152, 1024], replicated, may hold values from -0.1875 to 0.1875
- w_msg2: bfloat16 [1024, 1024], replicated, may hold values from -0.1875 to 0.1875
- w_input: bfloat16 [1024, 1536], replicated, may hold values from -0.1875 to 0.1875
- w_hidden: bfloat16 [512, 1536], replicated, may hold values from -0.25 to 0.25
Outputs:
- embeddings: bfloat16 [65536, 512], P(('owner', 'group'))
- new_memory: bfloat16 [262144, 512], P(('owner', 'group'))
Inputs may be any that keep to these rules, and one draw needn't show every extreme that they name: `dst_owner`: events of one device (aligned blocks of 512) name one owner at most 8 times; some owner is named exactly 8 times.
All inputs are finite; a program needn't handle non-finite values.
Results may differ from a plain program's by a relative error of at most 0.0043.
Values may be sent and summed in bfloat16 or wider, within the bound.
A program may use at most 128 MiB of HBM per device.

v0:
```python
import functools

import jax
import jax.numpy as jnp
from jax import lax
from jax.experimental import pallas as pl
from jax.experimental.pallas import tpu as pltpu
from jax.sharding import PartitionSpec as P

HEADS = 2
MESH = pl.DeviceIdType.MESH


def swap_kernel(x_ref, o_ref, send_sem, recv_sem, local_sem):
    groups = lax.axis_size("group")
    n = lax.axis_size("owner") * groups
    me = lax.axis_index("owner") * groups + lax.axis_index("group")
    barrier = pltpu.get_barrier_semaphore()

    def place(step):
        target = lax.rem(me + step, n)
        return target, (target // groups, lax.rem(target, groups))

    def greet(step, carry):
        _, device = place(step)
        pl.semaphore_signal(barrier, inc=1, device_id=device, device_id_type=MESH)
        return carry

    lax.fori_loop(1, n, greet, 0)
    pl.semaphore_wait(barrier, n - 1)
    own = pltpu.make_async_copy(x_ref.at[me], o_ref.at[me], local_sem)
    own.start()

    def send(step, carry):
        target, device = place(step)
        pltpu.make_async_remote_copy(
            src_ref=x_ref.at[target],
            dst_ref=o_ref.at[me],
            send_sem=send_sem,
            recv_sem=recv_sem,
            device_id=device,
            device_id_type=MESH,
        ).start()
        return carry

    lax.fori_loop(1, n, send, 0)
    own.wait()
    _, device = place(1)
    pltpu.make_async_remote_copy(
        src_ref=x_ref.at[pl.ds(0, n - 1)],
        dst_ref=o_ref.at[pl.ds(0, n - 1)],
        send_sem=send_sem,
        recv_sem=recv_sem,
        device_id=device,
        device_id_type=MESH,
    ).wait()


def swap(x, number):
    return pl.pallas_call(
        swap_kernel,
        out_shape=jax.ShapeDtypeStruct(x.shape, x.dtype),
        in_specs=[pl.BlockSpec(memory_space=pltpu.VMEM)],
        out_specs=pl.BlockSpec(memory_space=pltpu.VMEM),
        scratch_shapes=[pltpu.SemaphoreType.DMA] * 3,
        compiler_params=pltpu.CompilerParams(
            collective_id=number, has_side_effects=True, vmem_limit_bytes=16 << 20
        ),
    )(x)


def dot(a, b):
    return jnp.dot(a, b, preferred_element_type=jnp.float32)


def onehot(index, size):
    return (index[:, None] == jnp.arange(size, dtype=jnp.int32)[None, :]).astype(jnp.bfloat16)


def time_code(delta, time_freq):
    return jnp.cos(delta.astype(jnp.float32)[..., None] * time_freq).astype(jnp.bfloat16)


def per_device(
    memory,
    touched,
    src_pos,
    dst_owner,
    dst_slot,
    neighbors,
    ev_time,
    neigh_time,
    time_freq,
    w_query,
    w_key,
    w_value,
    w_out,
    w_msg1,
    w_msg2,
    w_input,
    w_hidden,
):
    devices = lax.axis_size(("owner", "group"))
    node_rows, width = memory.shape
    slots = touched.shape[2]
    msg_width = w_msg2.shape[1]
    count, neigh = neighbors.shape
    head_size = width // HEADS
    positions = devices * slots
    highest = lax.Precision.HIGHEST
    target = dst_owner[:, 0]
    dst_pos = target * slots + dst_slot
    dst_hot = onehot(dst_pos, positions)
    counts = jnp.sum(dst_hot.astype(jnp.float32), axis=0).astype(jnp.int32)
    note = jnp.concatenate(
        [
            touched.reshape(devices, slots),
            counts.reshape(devices, slots),
            jnp.zeros((devices, 128 - 2 * slots), jnp.int32),
        ],
        axis=1,
    )
    notes = swap(note.reshape(devices, 1, 128), 0)[:, 0, :]
    asked = notes[:, :slots].T.reshape(-1)
    asked_count = notes[:, slots : 2 * slots].T.reshape(-1)
    picked = dot(onehot(asked, node_rows), memory).astype(jnp.bfloat16)
    outgoing = picked.reshape(slots, devices, width // 128, 128).transpose(1, 0, 2, 3)
    table = swap(outgoing.reshape(devices, slots * width // 128, 128), 1)
    table = table.reshape(positions, width)

    src_mem = dot(onehot(src_pos, positions), table).astype(jnp.bfloat16)
    dst_mem = dot(dst_hot, table).astype(jnp.bfloat16)
    query = dot(dst_mem, w_query)
    key_table = dot(table, w_key[:width])
    value_table = dot(table, w_value[:width])
    code = time_code(ev_time[None, :] - neigh_time.T, time_freq)
    head_q = query.reshape(count, HEADS, head_size)
    head_k = key_table.reshape(positions, HEADS, head_size)
    head_v = value_table.reshape(positions, HEADS, head_size)
    full = jnp.einsum("ehd,phd->hep", head_q, head_k, precision=highest)
    key_code = w_key[width:].astype(jnp.float32).reshape(-1, HEADS, head_size)
    query_code = jnp.einsum("ehd,thd->eht", head_q, key_code, precision=highest)
    scores = []
    for k in range(neigh):
        hit = neighbors[:, k][:, None] == jnp.arange(positions, dtype=jnp.int32)[None, :]
        scores.append(
            jnp.sum(jnp.where(hit[None], full, 0.0), axis=2)
            + jnp.sum(query_code * code[k].astype(jnp.float32)[:, None, :], axis=2).T
        )
    weights = jax.nn.softmax(jnp.stack(scores) / jnp.sqrt(jnp.float32(head_size)), axis=0)
    spread = jnp.zeros_like(full)
    mixed = jnp.zeros((HEADS, count, code.shape[2]), jnp.float32)
    for k in range(neigh):
        hit = neighbors[:, k][:, None] == jnp.arange(positions, dtype=jnp.int32)[None, :]
        spread += jnp.where(hit[None], weights[k][:, :, None], 0.0)
        mixed += weights[k][:, :, None] * code[k].astype(jnp.float32)[None]
    value_code = w_value[width:].astype(jnp.float32).reshape(-1, HEADS, head_size)
    att = jnp.einsum("hep,phd->ehd", spread, head_v, precision=highest)
    att = att + jnp.einsum("het,thd->ehd", mixed, value_code, precision=highest)
    att = att.reshape(count, width).astype(jnp.bfloat16)
    emb = (dst_mem.astype(jnp.float32) + dot(att, w_out)).astype(jnp.bfloat16)
    joined = jnp.concatenate([src_mem, emb, time_code(ev_time, time_freq)], axis=1)
    hidden = jax.nn.relu(dot(joined, w_msg1)).astype(jnp.bfloat16)
    message = dot(hidden, w_msg2).astype(jnp.bfloat16)
    partial = dot(dst_hot.T, message).astype(jnp.bfloat16)
    inbox = swap(partial.reshape(devices, slots * msg_width // 128, 128), 2)
    inbox = inbox.reshape(devices, slots, msg_width).transpose(1, 0, 2).reshape(positions, -1)

    match = asked[:, None] == asked[None, :]
    total = dot(match.astype(jnp.bfloat16), inbox)
    number = jnp.sum(jnp.where(match, asked_count[None, :], 0), axis=1)
    agg = (total / jnp.maximum(number, 1).astype(jnp.float32)[:, None]).astype(jnp.bfloat16)
    gate_in = dot(agg, w_input)
    gate_state = dot(picked, w_hidden)
    gates = jax.nn.sigmoid(gate_in[:, : 2 * width] + gate_state[:, : 2 * width])
    reset, update = gates[:, :width], gates[:, width:]
    candidate = jnp.tanh(gate_in[:, 2 * width :] + reset * gate_state[:, 2 * width :])
    fresh = ((1.0 - update) * candidate + update * picked.astype(jnp.float32)).astype(jnp.bfloat16)
    order = jnp.arange(positions)
    first = jnp.sum(match & (order[None, :] < order[:, None]), axis=1) == 0
    leader = jnp.where(first & (number > 0), asked, -1)
    place = onehot(leader, node_rows).T
    moved = dot(place, fresh).astype(jnp.bfloat16)
    hit = jnp.sum(place.astype(jnp.float32), axis=1) > 0
    return emb, jnp.where(hit[:, None], moved, memory)


def solution(mesh):
    rows = P(("owner", "group"))
    in_specs = (rows,) * 8 + (P(),) * 9
    return jax.shard_map(
        per_device, mesh=mesh, in_specs=in_specs, out_specs=(rows, rows), check_vma=False
    )
```

profile of v0, /device:TPU:1, one launch (start us, length us, event | category | flops | bytes accessed | tf_op | source)
XLA Modules:
  0.0 173.3 jit_solution(9623134916518676638)
XLA Ops:
  0.6 0.9 convert_bitcast_fusion
  1.6 14.9 %cosine_convert_fusion = bf16[16,512,128]{1,2,0:T(8,128)(2,1)S(1)} fusion(f32[128]{0:T(128)} %param.25, f32[16,512]{1,0:T(8,128)S(1)} %convert_bitcast_fusion), kind=kLoop, calls=%fused_computation.3 | loop fusion | flops 2097152 | bytes 2130432 | tf_op jit(solution)/shard_map/convert_element_type | solution.py:81
  16.5 2.0 %fusion.190 = (f32[512,128]{0,1:T(8,128)S(1)}, f32[512,128]{0,1:T(8,128)}, f32[512,128]{0,1:T(8,128)}, f32[512,128]{0,1:T(8,128)}, f32[512,128]{0,1:T(8,128)}, /...) fusion(bf16[16,512,128]{1,2,0:T(8,128)(2,1)S(1)} %cosine_conver, ...), kind=kLoop, calls=%fused_computation.270 | loop fusion | flops 1048576 | bytes 6291456 | tf_op jit(solution)/shard_map/convert_element_type | solution.py:148
  19.2 16.5 %shard_map.176 = s32[128,1,128]{2,1,0:T(1,128)S(1)} custom-call(s32[128,1,128]{2,1,0:T(1,128)S(1)} %bitcast.223), custom_call_target="tpu_custom_call" | custom-call | tf_op jit(solution)/shard_map/pallas_call | solution.py:60
  36.4 3.7 %fusion.53 = bf16[512,512]{1,0:T(8,128)(2,1)} fusion(bf16[2048,512]{1,0:T(8,128)(2,1)} %param.17, s32[512]{0:T(512)S(1)} %bitcast.233), kind=kOutput, calls=%fused_computation.81 | convolution fusion | flops 1075052544 | bytes 2623488 | tf_op jit(solution)/shard_map/dot_general | solution.py:73
  40.1 2.0 %reshape.530 = bf16[4,128,4,128]{3,2,1,0:T(4,128)(2,1)} reshape(bf16[512,512]{1,0:T(8,128)(2,1)} %fusion.53) | data formatting | bytes 1048576 | tf_op jit(solution)/shard_map/reshape | solution.py:127
  42.1 1.2 copy.42
  43.3 15.8 %shard_map.177 = bf16[128,16,128]{2,1,0:T(8,128)(2,1)S(1)} custom-call(bf16[128,16,128]{2,1,0:T(8,128)(2,1)S(1)} %bitcast.221), custom_call_target="tpu_custom_call" | custom-call | tf_op jit(solution)/shard_map/pallas_call | solution.py:60
  59.1 0.8 copy-done.1
  59.9 2.1 %reshape.532 = bf16[512,512]{1,0:T(8,128)(2,1)} reshape(bf16[128,16,128]{2,1,0:T(8,128)(2,1)} %copy-done.1) | data formatting | bytes 1048576 | tf_op jit(solution)/shard_map/reshape | solution.py:129
  62.0 1.7 convolution_convert_fusion.3
  63.8 0.8 copy-done.7
  64.6 2.5 %fusion.197 = f32[512,512]{0,1:T(8,128)} fusion(bf16[512,512]{0,1:T(8,128)(2,1)S(1)} %convolution_convert_fusion.3, bf16[512,512]{1,0:T(8,128)(2,1)} %param.26), kind=kOutput, calls=%fused_computation.320 | convolution fusion | flops 268435456 | bytes 2097152 | tf_op jit(solution)/shard_map/dot_general | solution.py:73
  67.1 0.7 copy.62
  67.8 4.0 %multiply_reduce_fusion = (f32[2,512]{1,0:T(2,128)S(1)}, f32[2,512]{1,0:T(2,128)S(1)}, f32[2,512]{1,0:T(2,128)S(1)}, f32[2,512]{1,0:T(2,128)S(1)}, f32[2,512]{1,...) fusion(f32[512,128]{0,1:T(8,128)} %get-tuple-element.43, ...), kind=kOutput, calls=%fused_computation.185 | convolution fusion | flops 406831104 | bytes 5439488 | tf_op jit(solution)/shard_map/ehd,thd->eht/dot_general | solution.py:142
  71.8 1.1 iota_compare_fusion.19
  73.0 1.1 iota_compare_fusion.21
  74.1 1.1 iota_compare_fusion.23
  75.2 1.1 iota_compare_fusion.25
  76.3 1.1 iota_compare_fusion.27
  77.5 1.1 iota_compare_fusion.13
  78.6 1.1 iota_compare_fusion.15
  79.7 1.1 iota_compare_fusion.17
  80.8 2.2 %reshape.555 = bf16[512,512,1]{1,0,2:T(8,128)(2,1)} reshape(bf16[128,16,128]{2,1,0:T(8,128)(2,1)} %copy-done.1) | data formatting | bytes 1048576 | tf_op jit(solution)/shard_map/reshape | solution.py:129
  82.9 1.9 %slice_bitcast_fusion = bf16[512,512]{0,1:T(8,128)(2,1)} fusion(bf16[640,512]{1,0:T(8,128)(2,1)} %param.27), kind=kLoop, calls=%fused_computation.201 | loop fusion | bytes 1048576 | tf_op jit(solution)/shard_map/dot_general | solution.py:73
  84.8 2.1 %copy.44 = bf16[512,512]{1,0:T(8,128)(2,1)} copy(bf16[512,512]{0,1:T(8,128)(2,1)} %slice_bitcast_fusion) | data formatting | bytes 1048576 | tf_op jit(solution)/shard_map/dot_general | solution.py:73
  86.9 1.8 %fusion.198 = f32[512,2,256]{2,0,1:T(8,128)S(1)} fusion(bf16[512,512,1]{1,0,2:T(8,128)(2,1)} %reshape.555, bf16[2,256,512]{2,1,0:T(8,128)(2,1)} %bitcast.228), kind=kOutput, calls=%fused_computation.321 | convolution fusion | flops 268435456 | bytes 2097152 | tf_op jit(solution)/shard_map/dot_general | solution.py:73
  88.8 8.1 %select_reduce_fusion = (f32[2,512]{1,0:T(2,128)S(1)}, f32[2,512]{1,0:T(2,128)S(1)}, f32[2,512]{1,0:T(2,128)S(1)}, f32[2,512]{1,0:T(2,128)S(1)}, f32[2,512]{1,0:...) fusion(pred[512,512]{0,1:T(8,128)(4,1)} %get-tuple-element.94, ...), kind=kOutput, calls=%fused_computation.50 | convolution fusion | flops 1627373568 | bytes 6356992 | tf_op jit(solution)/shard_map/ehd,phd->hep/dot_general | solution.py:140
  98.0 0.8 slice_bitcast_fusion.1
  98.8 2.1 %copy.43 = bf16[512,512]{1,0:T(8,128)(2,1)} copy(bf16[512,512]{0,1:T(8,128)(2,1)} %slice_bitcast_fusion.1) | data formatting | bytes 1048576 | tf_op jit(solution)/shard_map/dot_general | solution.py:73
  101.0 1.8 %fusion.196 = f32[512,2,256]{0,2,1:T(8,128)S(1)} fusion(bf16[512,512,1]{1,0,2:T(8,128)(2,1)} %reshape.555, bf16[2,256,512]{2,1,0:T(8,128)(2,1)} %bitcast.227), kind=kOutput, calls=%fused_computation.319 | convolution fusion | flops 268435456 | bytes 2097152 | tf_op jit(solution)/shard_map/dot_general | solution.py:73
  102.9 8.7 %fusion.48 = f32[512,2,256]{0,2,1:T(8,128)} fusion(f32[512,2,256]{0,2,1:T(8,128)S(1)} %fusion.196, f32[2,512]{1,0:T(2,128)S(1)} %get-tuple-element.61, f32[2,512]{1,0:T(2,128)S(1)} %get-tuple-element.62, f32[2,512]{1,0:T(2,128)} %get-tuple-element.63, f32[2,512]{1,0:T(2,128)} %get-tuple-element.64, f32[2,512]{1,0:T(2,128)} %get-tuple-element.65, ...), kind=kOutput, calls=%fused_computation.76 | convolution fusion | flops 1626865664 | bytes 6356992 | tf_op jit(solution)/shard_map/hep,phd->ehd/dot_general | solution.py:158
  111.6 0.8 copy.51
  112.3 3.9 %fusion.51 = bf16[512,2,256]{0,2,1:T(8,128)(2,1)S(1)} fusion(f32[512,2,256]{0,2,1:T(8,128)} %fusion.48, bf16[128,2,256]{0,2,1:T(8,128)(2,1)} %bitcast.230, f32[2,512]{1,0:T(2,128)S(1)} %get-tuple-element.61, f32[2,512]{1,0:T(2,128)S(1)} %get-tuple-element.62, f32[2,512]{1,0:T(2,128)} %get-tuple-element.63, f32[2,512]{1,0:T(2,128)} %get-tuple-element.64, ...), kind=kOutput, calls=%fused_computation.79 | convolution fusion | flops 407240704 | bytes 5963776 | tf_op jit(solution)/shard_map/het,thd->ehd/dot_general | solution.py:159
  118.0 0.9 cosine_convert_fusion.1
  118.9 2.5 %maximum_convert_fusion = bf16[512,1024]{1,0:T(8,128)(2,1)} fusion(bf16[1152,1024]{1,0:T(8,128)(2,1)S(1)} %copy-done.34, bf16[512,128]{0,1:T(8,128)(2,1)S(1)} %cosine_convert_fusion.1, bf16[512,512]{0,1:T(8,128)(2,1)S(1)} %fusion.52, bf16[512,512]{0,1:T(8,128)(2,1)S(1)} %convolution_convert_fusion.2), kind=kOutput, calls=%fused_computation.16 | convolution fusion | flops 1212547072 | bytes 4587520 | tf_op jit(solution)/shard_map/dot_general | solution.py:73
  121.4 4.7 %convolution_convert_fusion = bf16[512,1024]{1,0:T(8,128)(2,1)} fusion(bf16[512,1024]{1,0:T(8,128)(2,1)} %maximum_convert_fusion, bf16[1024,1024]{1,0:T(8,128)(2,1)} %param.31, s32[512]{0:T(512)S(1)} %copy-done.29), kind=kOutput, calls=%fused_computation.71 | convolution fusion | flops 1611923456 | bytes 4196352 | tf_op jit(solution)/shard_map/dot_general | solution.py:73
  126.2 2.3 %reshape.536.x_ref = bf16[128,32,128]{2,1,0:T(8,128)(2,1)} reshape(bf16[512,1024]{1,0:T(8,128)(2,1)} %convolution_convert_fusion) | data formatting | bytes 2097152 | tf_op jit(solution)/shard_map/reshape | solution.py:166
  128.4 1.2 copy-done.2
  129.7 22.5 %shard_map.178 = bf16[128,32,128]{2,1,0:T(8,128)(2,1)S(1)} custom-call(bf16[128,32,128]{2,1,0:T(8,128)(2,1)S(1)} %copy-done.2), custom_call_target="tpu_custom_call" | custom-call | tf_op jit(solution)/shard_map/pallas_call | solution.py:60
  152.2 1.0 copy-done.3
  153.1 2.2 %reshape.537 = bf16[128,4,1024]{2,1,0:T(4,128)(2,1)} reshape(bf16[128,32,128]{2,1,0:T(8,128)(2,1)} %copy-done.3) | data formatting | bytes 2097152 | tf_op jit(solution)/shard_map/reshape | solution.py:167
  155.3 2.5 %copy.54 = bf16[128,4,1024]{2,0,1:T(8,128)(2,1)} copy(bf16[128,4,1024]{2,1,0:T(4,128)(2,1)} %reshape.537) | data formatting | bytes 2097152 | tf_op jit(solution)/shard_map/reshape | solution.py:167
  158.3 5.3 %fusion.55 = f32[512,1536]{1,0:T(8,128)} fusion(bf16[1024,1536]{1,0:T(8,128)(2,1)S(1)} %copy-done, bf16[512,1024]{1,0:T(8,128)(2,1)} %bitcast.229, f32[512]{0:T(512)S(1)} %get-tuple-element.92, s32[512]{0:T(512)S(1)} %bitcast.235), kind=kOutput, calls=%fused_computation.82 | convolution fusion | flops 2148794368 | bytes 7344128 | tf_op jit(solution)/shard_map/dot_general | solution.py:73
  163.6 2.7 %fusion.199 = f32[512,1536]{1,0:T(8,128)S(1)} fusion(bf16[512,512]{1,0:T(8,128)(2,1)} %fusion.53, bf16[512,1536]{1,0:T(8,128)(2,1)} %param.33), kind=kOutput, calls=%fused_computation.322 | convolution fusion | flops 805306368 | bytes 5242880 | tf_op jit(solution)/shard_map/dot_general | solution.py:73
  166.3 0.8 fusion.8
  168.1 3.2 %fusion.4 = bf16[2048,512]{1,0:T(8,128)(2,1)} fusion(bf16[2048,512]{1,0:T(8,128)(2,1)S(1)} %copy-done.35, s32[512]{0:T(512)S(1)} %get-tuple-element.93, pred[2048]{0:T(1024)(128)(4,1)S(1)} %broadcast_compare_fusion, f32[512,1536]{1,0:T(8,128)S(1)} %fusion.199, f32[512,1024]{1,0:T(8,128)S(1)} %fusion.8, f32[512,1536]{1,0:T(8,128)S(1)} %copy-done.9, ...), kind=kOutput, calls=%fused_computation.9 | convolution fusion | flops 1078984704 | bytes 8916992 | tf_op jit(solution)/shard_map/dot_general | solution.py:73
  171.3 2.0 %copy.55 = bf16[512,512]{1,0:T(8,128)(2,1)} copy(bf16[512,512]{0,1:T(8,128)(2,1)} %copy-done.6) | data formatting | bytes 1048576
  (114 shorter events, 5.6 us)
Async XLA Ops:
  0.6 157.7 %copy-start = (bf16[1024,1536]{1,0:T(8,128)(2,1)S(1)}, bf16[1024,1536]{1,0:T(8,128)(2,1)}, u32[]{:S(2)}) copy-start(bf16[1024,1536]{1,0:T(8,128)(2,1)} %param.32) | copy-start | bytes 9437188
  16.5 2.0 %copy-start.33 = (s32[512,1]{0,1:T(1,128)S(1)}, s32[512,1]{0,1:T(1,128)}, u32[]{:S(2)}) copy-start(s32[512,1]{0,1:T(1,128)} %param.20) | copy-start | bytes 6148
  16.5 2.0 %copy-start.31 = (s32[512]{0:T(512)S(1)}, s32[512]{0:T(512)}, u32[]{:S(2)}) copy-start(s32[512]{0:T(512)} %param.21) | copy-start | bytes 6148
  16.5 2.3 %copy-start.32 = (s32[1,128,4]{1,2,0:T(4,128)S(1)}, s32[1,128,4]{1,2,0:T(4,128)}, u32[]{:S(2)}) copy-start(s32[1,128,4]{1,2,0:T(4,128)} %param.18) | copy-start | bytes 6148
  18.6 43.5 %copy-start.28 = (s32[512]{0:T(512)}, s32[512]{0:T(512)S(1)}, u32[]{:S(2)}) copy-start(s32[512]{0:T(512)S(1)} %add.159) | copy-start | bytes 6148
  59.1 0.8 copy-start.1
  62.0 5.0 %slice-start = ((bf16[640,512]{1,0:T(8,128)(2,1)}), bf16[128,512]{1,0:T(8,128)(2,1)S(1)}, s32[]{:S(2)}) async-start(bf16[640,512]{1,0:T(8,128)(2,1)} %param.27), calls=%async_computation | async-start | bytes 262144 | tf_op jit(solution)/shard_map/slice | solution.py:141
  63.8 0.8 copy-start.7
  67.8 4.0 %copy-start.26 = (s32[512,16]{0,1:T(8,128)S(1)}, s32[512,16]{0,1:T(8,128)}, u32[]{:S(2)}) copy-start(s32[512,16]{0,1:T(8,128)} %param.22) | copy-start | bytes 98308
  86.9 1.8 %copy-start.4 = (f32[512,512]{0,1:T(8,128)S(1)}, f32[512,512]{0,1:T(8,128)}, u32[]{:S(2)}) copy-start(f32[512,512]{0,1:T(8,128)} %fusion.197) | copy-start | bytes 3145732
  86.9 1.8 %copy-start.13 = (pred[512,512]{0,1:T(8,128)(4,1)S(1)}, pred[512,512]{0,1:T(8,128)(4,1)}, u32[]{:S(2)}) copy-start(pred[512,512]{0,1:T(8,128)(4,1)} %get-tuple-element.100) | copy-start | bytes 786436
  86.9 1.9 %copy-start.15 = (pred[512,512]{0,1:T(8,128)(4,1)S(1)}, pred[512,512]{0,1:T(8,128)(4,1)}, u32[]{:S(2)}) copy-start(pred[512,512]{0,1:T(8,128)(4,1)} %get-tuple-element.101) | copy-start | bytes 786436
  86.9 1.9 %copy-start.17 = (pred[512,512]{0,1:T(8,128)(4,1)S(1)}, pred[512,512]{0,1:T(8,128)(4,1)}, u32[]{:S(2)}) copy-start(pred[512,512]{0,1:T(8,128)(4,1)} %get-tuple-element.102) | copy-start | bytes 786436
  86.9 1.9 %copy-start.19 = (pred[512,512]{0,1:T(8,128)(4,1)S(1)}, pred[512,512]{0,1:T(8,128)(4,1)}, u32[]{:S(2)}) copy-start(pred[512,512]{0,1:T(8,128)(4,1)} %get-tuple-element.103) | copy-start | bytes 786436
  88.8 9.2 %copy-start.10 = (bf16[640,512]{1,0:T(8,128)(2,1)S(1)}, bf16[640,512]{1,0:T(8,128)(2,1)}, u32[]{:S(2)}) copy-start(bf16[640,512]{1,0:T(8,128)(2,1)} %param.28) | copy-start | bytes 1966084
  100.9 1.9 %copy-start.14 = (pred[512,512]{0,1:T(8,128)(4,1)S(1)}, pred[512,512]{0,1:T(8,128)(4,1)}, u32[]{:S(2)}) copy-start(pred[512,512]{0,1:T(8,128)(4,1)} %get-tuple-element.100) | copy-start | bytes 786436
  100.9 1.9 %copy-start.16 = (pred[512,512]{0,1:T(8,128)(4,1)S(1)}, pred[512,512]{0,1:T(8,128)(4,1)}, u32[]{:S(2)}) copy-start(pred[512,512]{0,1:T(8,128)(4,1)} %get-tuple-element.101) | copy-start | bytes 786436
  100.9 1.9 %copy-start.18 = (pred[512,512]{0,1:T(8,128)(4,1)S(1)}, pred[512,512]{0,1:T(8,128)(4,1)}, u32[]{:S(2)}) copy-start(pred[512,512]{0,1:T(8,128)(4,1)} %get-tuple-element.102) | copy-start | bytes 786436
  100.9 1.9 %copy-start.20 = (pred[512,512]{0,1:T(8,128)(4,1)S(1)}, pred[512,512]{0,1:T(8,128)(4,1)}, u32[]{:S(2)}) copy-start(pred[512,512]{0,1:T(8,128)(4,1)} %get-tuple-element.103) | copy-start | bytes 786436
  100.9 1.9 %copy-start.21 = (pred[512,512]{0,1:T(8,128)(4,1)S(1)}, pred[512,512]{0,1:T(8,128)(4,1)}, u32[]{:S(2)}) copy-start(pred[512,512]{0,1:T(8,128)(4,1)} %get-tuple-element.104) | copy-start | bytes 786436
  100.9 1.9 %copy-start.22 = (pred[512,512]{0,1:T(8,128)(4,1)S(1)}, pred[512,512]{0,1:T(8,128)(4,1)}, u32[]{:S(2)}) copy-start(pred[512,512]{0,1:T(8,128)(4,1)} %get-tuple-element.105) | copy-start | bytes 786436
  100.9 1.9 %copy-start.23 = (pred[512,512]{0,1:T(8,128)(4,1)S(1)}, pred[512,512]{0,1:T(8,128)(4,1)}, u32[]{:S(2)}) copy-start(pred[512,512]{0,1:T(8,128)(4,1)} %get-tuple-element.106) | copy-start | bytes 786436
  100.9 1.9 %copy-start.24 = (pred[512,512]{0,1:T(8,128)(4,1)S(1)}, pred[512,512]{0,1:T(8,128)(4,1)}, u32[]{:S(2)}) copy-start(pred[512,512]{0,1:T(8,128)(4,1)} %get-tuple-element.107) | copy-start | bytes 786436
  102.8 8.7 %slice-start.1 = ((bf16[640,512]{1,0:T(8,128)(2,1)}), bf16[128,512]{1,0:T(8,128)(2,1)S(1)}, s32[]{:S(2)}) async-start(bf16[640,512]{1,0:T(8,128)(2,1)} %param.28), calls=%async_computation.1 | async-start | bytes 262144 | tf_op jit(solution)/shard_map/slice | solution.py:157
  112.3 4.0 %copy-start.8 = (bf16[512,512]{0,1:T(8,128)(2,1)S(1)}, bf16[512,512]{0,1:T(8,128)(2,1)}, u32[]{:S(2)}) copy-start(bf16[512,512]{0,1:T(8,128)(2,1)} %copy-done.7) | copy-start | bytes 1572868
  112.3 4.0 %copy-start.12 = (bf16[512,512]{1,0:T(8,128)(2,1)S(1)}, bf16[512,512]{1,0:T(8,128)(2,1)}, u32[]{:S(2)}) copy-start(bf16[512,512]{1,0:T(8,128)(2,1)} %param.29) | copy-start | bytes 1572868
  112.3 4.5 %copy-start.36 = (s32[512]{0:T(512)S(1)}, s32[512]{0:T(512)}, u32[]{:S(2)}) copy-start(s32[512]{0:T(512)} %param.19) | copy-start | bytes 6148
  116.3 1.0 copy-start.11
  116.3 1.7 copy-start.27
  116.3 1.7 copy-start.30
  116.3 2.6 %copy-start.34 = (bf16[1152,1024]{1,0:T(8,128)(2,1)S(1)}, bf16[1152,1024]{1,0:T(8,128)(2,1)}, u32[]{:S(2)}) copy-start(bf16[1152,1024]{1,0:T(8,128)(2,1)} %param.30) | copy-start | bytes 7077892
  117.3 1.6 copy-start.6
  118.9 2.5 %copy-start.29 = (s32[512]{0:T(512)S(1)}, s32[512]{0:T(512)}, u32[]{:S(2)}) copy-start(s32[512]{0:T(512)} %copy-done.28) | copy-start | bytes 6148
  128.4 1.2 copy-start.2
  152.2 1.0 copy-start.3
  153.1 4.7 %copy-start.25 = (s32[4,128]{0,1:T(8,128)S(1)}, s32[4,128]{0,1:T(8,128)}, u32[]{:S(2)}) copy-start(s32[4,128]{0,1:T(8,128)} %get-tuple-element.58) | copy-start | bytes 6148
  163.6 2.7 %copy-start.9 = (f32[512,1536]{1,0:T(8,128)S(1)}, f32[512,1536]{1,0:T(8,128)}, u32[]{:S(2)}) copy-start(f32[512,1536]{1,0:T(8,128)} %fusion.55) | copy-start | bytes 9437188
  166.3 1.3 copy-start.5
  166.3 1.8 %copy-start.35 = (bf16[2048,512]{1,0:T(8,128)(2,1)S(1)}, bf16[2048,512]{1,0:T(8,128)(2,1)}, u32[]{:S(2)}) copy-start(bf16[2048,512]{1,0:T(8,128)(2,1)} %param.17) | copy-start | bytes 6291460
where the time goes:
time: 174 us; the launch traced here: 173 us
  matrix products  55.7 us (32%)
  Pallas kernels  54.7 us (31%)
  local copies, waits for them, and re-layouts  31.5 us (18%)
  other arithmetic  30 us (17%)
    pallas_call x3, Pallas kernels, swap(): pl.pallas_call(swap_kernel, out_shape=jax.ShapeDtypeStruct(x.shape, x.dty...  54.7 us
    dot_general x12, matrix products, dot(): return jnp.dot(a, b, preferred_element_type=jnp.float32)  31 us
    convert_element_type x2, other arithmetic, time_code(): jnp.cos(delta.astype(jnp.float32)[..., None] * time_freq)  15.9 us
    eq x8, other arithmetic, per_device(): neighbors[:, k][:, None] == jnp.arange(positions, dtype=jnp.int32)[None, :]  8.94 us
    dot_general x1, matrix products, per_device(): att = jnp.einsum('hep,phd->ehd', spread, head_v, precision=highest)  8.7 us
    dot_general x1, matrix products, per_device(): full = jnp.einsum('ehd,phd->hep', head_q, head_k, precision=highest)  8.15 us
    unnamed x77, local copies, waits for them, and re-layouts  7.75 us
    dot_general x4, local copies, waits for them, and re-layouts, dot(): return jnp.dot(a, b, preferred_element_type=jnp.float32)  6.84 us

commit v1 on v0

v1 whole, which is shorter than its diff:
```python
import jax
import jax.numpy as jnp
from jax import lax
from jax.experimental import pallas as pl
from jax.experimental.pallas import tpu as pltpu
from jax.sharding import PartitionSpec as P

HEADS = 2
MESH = pl.DeviceIdType.MESH
f32, bf16, i32 = jnp.float32, jnp.bfloat16, jnp.int32
COS = (
    0.9999992251396179,
    -0.499994158744812,
    0.041659727692604065,
    -0.00138586456887424,
    2.4201255655498244e-05,
    -2.196603787751883e-07,
)
NN = (((1,), (0,)), ((), ()))
NT = (((1,), (1,)), ((), ()))


def dot(a, b, dims=NN):
    return lax.dot_general(a, b, dims, preferred_element_type=f32)


def iota(shape, axis):
    return lax.broadcasted_iota(i32, shape, axis)


def hot(mask):
    return jnp.where(mask, 1.0, 0.0).astype(bf16)


def split(x):
    high = x.astype(bf16)
    return high, (x - high.astype(f32)).astype(bf16)


def cosine(x):
    turns = jnp.floor(x * 0.15915494309189535 + 0.5)
    r = (x - turns * 6.28125) - turns * 0.0019353071795864769
    r = r * r
    y = COS[-1] * r + COS[-2]
    for c in COS[-3::-1]:
        y = y * r + c
    return y


def window_kernel(
    ints,
    cols,
    asks,
    freq_col,
    freq_row,
    memory_hbm,
    w_hidden_hbm,
    w_query_hbm,
    w_key_hbm,
    w_value_hbm,
    w_out_hbm,
    w_msg1_hbm,
    w_msg2_hbm,
    w_input_hbm,
    emb_hbm,
    fresh_out,
    leader_out,
    memory,
    w_hidden,
    w_query,
    w_key,
    w_value,
    w_out,
    w_msg1,
    w_msg2,
    w_input,
    load_sem,
    emb_sem,
    note,
    note_in,
    relay,
    notes,
    note_sem,
    own_sem,
    stage,
    outbox,
    inbox,
    table_sem,
    part_out,
    part_in,
    part_sem,
    code,
    picked,
    state,
    value_t,
    match_ref,
    share,
    ev_code,
    src_hot,
    dst_hot,
    dst_hot_t,
    table,
    full,
    query_code,
    spread_hi,
    spread_lo,
    emb,
    partial,
    gates,
):
    groups, owners = 8, 16
    n = groups * owners
    o, g = lax.axis_index("owner"), lax.axis_index("group")
    me = o * groups + g
    neigh, te, width = 16, 128, 512

    barrier = pltpu.get_barrier_semaphore()
    for step in range(1, groups):
        pl.semaphore_signal(
            barrier, inc=1, device_id=(o, (g + step) & (groups - 1)), device_id_type=MESH
        )
    for step in range(1, owners):
        pl.semaphore_signal(
            barrier, inc=1, device_id=((o + step) & (owners - 1), g), device_id_type=MESH
        )
    loads = []
    for number, (source, target) in enumerate(
        (
            (memory_hbm, memory),
            (w_hidden_hbm, w_hidden),
            (w_value_hbm, w_value),
            (w_query_hbm, w_query),
            (w_key_hbm, w_key),
            (w_out_hbm, w_out),
            (w_msg1_hbm, w_msg1),
            (w_msg2_hbm, w_msg2),
            (w_input_hbm, w_input),
        )
    ):
        load = pltpu.make_async_copy(source, target, load_sem.at[number])
        load.start()
        loads.append(load)

    row = iota((n, 1), 0)
    device = ((row & (owners - 1)) * groups) + (row // owners)
    owner_hot = hot(device == ints[34:35, :])
    slot_hot = hot(iota((n, 512), 0) == ints[35:36, :] + 4)
    note[...] = asks[...] + dot(owner_hot, slot_hot, NT).astype(i32)
    pl.semaphore_wait(barrier, groups + owners - 2)

    def note_part(index):
        return pl.ds(pl.multiple_of(index * owners, owners), owners)

    own = pltpu.make_async_copy(note.at[note_part(g)], note_in.at[note_part(g)], own_sem.at[0])
    own.start()
    for step in range(1, groups):
        peer = (g + step) & (groups - 1)
        pltpu.make_async_remote_copy(
            src_ref=note.at[note_part(peer)],
            dst_ref=note_in.at[note_part(g)],
            send_sem=note_sem.at[0],
            recv_sem=note_sem.at[1],
            device_id=(o, peer),
            device_id_type=MESH,
        ).start()

    def make_codes(first):
        def codes(i, carry):
            rows = pl.ds(pl.multiple_of(i * 16, 16), 16)
            freq = freq_col[rows, :]
            for k in range(first, first + neigh // 2):
                delta = ints[k + neigh : k + neigh + 1, :].astype(f32)
                code[k, rows, :] = cosine(freq * delta).astype(bf16).astype(f32)
            return carry

        lax.fori_loop(0, te // 16, codes, 0)

    make_codes(0)
    own.wait()
    some = (groups - 1) * owners
    pltpu.make_async_remote_copy(
        src_ref=note.at[pl.ds(0, some)],
        dst_ref=note_in.at[pl.ds(0, some)],
        send_sem=note_sem.at[0],
        recv_sem=note_sem.at[1],
        device_id=(o, (g + 1) & (groups - 1)),
        device_id_type=MESH,
    ).wait()
    for owner in range(owners):
        relay[owner] = note_in[pl.ds(owner, groups, stride=owners), :]
    own = pltpu.make_async_copy(relay.at[o], notes.at[o], own_sem.at[1])
    own.start()
    for step in range(1, owners):
        peer = (o + step) & (owners - 1)
        pltpu.make_async_remote_copy(
            src_ref=relay.at[peer],
            dst_ref=notes.at[o],
            send_sem=note_sem.at[2],
            recv_sem=note_sem.at[3],
            device_id=(peer, g),
            device_id_type=MESH,
        ).start()
    make_codes(neigh // 2)
    own.wait()
    pltpu.make_async_remote_copy(
        src_ref=relay.at[pl.ds(0, owners - 1)],
        dst_ref=notes.at[pl.ds(0, owners - 1)],
        send_sem=note_sem.at[2],
        recv_sem=note_sem.at[3],
        device_id=((o + 1) & (owners - 1), g),
        device_id_type=MESH,
    ).wait()
    known = notes[...].reshape(n, 128)
    known_t = known.astype(f32).T.astype(i32)

    loads[0].wait()
    for s in range(4):
        rows = dot(hot(iota((n, 2048), 1) == known[:, s : s + 1]), memory[...])
        picked[s * n : (s + 1) * n, :] = rows.astype(bf16)
        for c in range(4):
            stage[pl.ds(s * 4 + c, n, stride=16), :] = rows[:, c * 128 : (c + 1) * 128]
    outbox[...] = stage[...].astype(bf16).reshape(n, 16, 128)

    def send_all(source, target, send_sem, recv_sem):
        def send(step, carry):
            peer = (me + step) & (n - 1)
            pltpu.make_async_remote_copy(
                src_ref=source.at[peer],
                dst_ref=target.at[me],
                send_sem=send_sem,
                recv_sem=recv_sem,
                device_id=(peer // groups, peer & (groups - 1)),
                device_id_type=MESH,
            ).start()
            return carry

        lax.fori_loop(1, n, send, 0)

    def all_sent(source, target, send_sem, recv_sem):
        return pltpu.make_async_remote_copy(
            src_ref=source.at[pl.ds(0, n - 1)],
            dst_ref=target.at[pl.ds(0, n - 1)],
            send_sem=send_sem,
            recv_sem=recv_sem,
            device_id=(o, (g + 1) & (groups - 1)),
            device_id_type=MESH,
        )

    own = pltpu.make_async_copy(outbox.at[me], inbox.at[me], own_sem.at[2])
    own.start()
    send_all(outbox, inbox, table_sem.at[0], table_sem.at[1])

    loads[1].wait()
    state[...] = dot(picked[...], w_hidden[...])
    loads[2].wait()
    value_t[...] = w_value[...].astype(f32).T.astype(bf16)
    asked_col = jnp.concatenate([known[:, s : s + 1] for s in range(4)], axis=0)
    count_col = jnp.concatenate([known[:, s + 4 : s + 5] for s in range(4)], axis=0)
    asked_row = jnp.concatenate([known_t[s : s + 1, :] for s in range(4)], axis=1)
    count_row = jnp.concatenate([known_t[s + 4 : s + 5, :] for s in range(4)], axis=1)
    match = asked_col == asked_row
    match_ref[...] = hot(match)
    number = jnp.sum(jnp.where(match, count_row.astype(f32), 0.0), axis=1, keepdims=True)
    share[...] = jnp.broadcast_to(1.0 / jnp.maximum(number, 1.0), share.shape)
    number_row = jnp.sum(jnp.where(match, count_col.astype(f32), 0.0), axis=0, keepdims=True)
    earlier = match & (iota((512, 512), 0) < iota((512, 512), 1))
    earlier = jnp.sum(jnp.where(earlier, 1.0, 0.0), axis=0, keepdims=True)
    leader = jnp.where((earlier == 0.0) & (number_row > 0.0), asked_row, -1)
    leader_out[...] = jnp.broadcast_to(leader, leader_out.shape)
    ev_code[...] = cosine(cols[:, 2:3].astype(f32) * freq_row[...]).astype(bf16)
    src_hot[...] = hot(iota((512, 512), 1) == cols[:, 0:1])
    dst_hot[...] = hot(iota((512, 512), 1) == cols[:, 1:2])
    dst_hot_t[...] = hot(iota((512, 512), 0) == ints[33:34, :])

    own.wait()
    all_sent(outbox, inbox, table_sem.at[0], table_sem.at[1]).wait()
    stage[...] = inbox[...].reshape(n * 16, 128).astype(f32)
    for c in range(4):
        table[:, c * 128 : (c + 1) * 128] = stage[pl.ds(c, 512, stride=4), :].astype(bf16)

    dst_mem = dot(dst_hot[...], table[...])
    src_mem = dot(src_hot[...], table[...]).astype(bf16)
    loads[3].wait()
    loads[4].wait()
    query = dot(dst_mem.astype(bf16), w_query[...]) * (1.0 / 16.0)
    query_hi, query_lo = split(query)
    key_hi, key_lo = split(dot(table[...], w_key[:width, :]))
    for h in range(HEADS):
        part = slice(h * 256, h * 256 + 256)
        full[h] = (
            dot(key_hi[:, part], query_hi[:, part], NT)
            + dot(key_hi[:, part], query_lo[:, part], NT)
            + dot(key_lo[:, part], query_hi[:, part], NT)
        )
        query_code[h] = dot(w_key[width:, part], query_hi[:, part], NT) + dot(
            w_key[width:, part], query_lo[:, part], NT
        )
    val_hi, val_lo = split(dot(value_t[:, :width], table[...], NT))

    def attend(piece, carry):
        lanes = pl.ds(pl.multiple_of(piece * 128, 128), 128)
        near = ints[0:neigh, lanes]
        near8 = [jnp.broadcast_to(near[k : k + 1, :], (8, 128)) for k in range(neigh)]
        sub = iota((8, 128), 0)

        def look(i, sums):
            sums = list(sums)
            for u in range(4):
                base = pl.multiple_of(i * 32 + u * 8, 8)
                place = sub + base
                first = full[0, pl.ds(base, 8), lanes]
                second = full[1, pl.ds(base, 8), lanes]
                for k in range(neigh):
                    mask = place == near8[k]
                    sums[k] = jnp.where(mask, first, sums[k])
                    sums[neigh + k] = jnp.where(mask, second, sums[neigh + k])
            return tuple(sums)

        zero = jnp.zeros((8, 128), f32)
        sums = list(lax.fori_loop(0, 16, look, (zero,) * (2 * neigh)))
        rows = [[], []]
        for h in range(HEADS):
            mine = query_code[h, :, lanes]
            for k in range(neigh):
                prod = (code[k, :, lanes] * mine).reshape(te // 8, 8, 128)
                prod = jnp.sum(prod, axis=0) + sums[h * neigh + k]
                rows[h].append(jnp.sum(prod, axis=0, keepdims=True))
        whole = []
        weights = []
        for h in range(HEADS):
            score = jnp.concatenate(rows[h], axis=0)
            score = jnp.exp(score - jnp.max(score, axis=0, keepdims=True))
            weight = score / jnp.sum(score, axis=0, keepdims=True)
            total = jnp.zeros((neigh, 128), f32)
            for k in range(neigh):
                total += jnp.where(near == near[k : k + 1, :], weight[k : k + 1, :], 0.0)
            weights.append(weight)
            whole.append([jnp.broadcast_to(total[k : k + 1, :], (16, 128)) for k in range(neigh)])
        near16 = [jnp.broadcast_to(near[k : k + 1, :], (16, 128)) for k in range(neigh)]
        sub16 = iota((16, 128), 0)

        def put(i, carry):
            base = pl.multiple_of(i * 16, 16)
            place = sub16 + base
            both = [jnp.zeros((16, 128), f32)] * HEADS
            for k in range(neigh):
                mask = place == near16[k]
                for h in range(HEADS):
                    both[h] = jnp.where(mask, whole[h][k], both[h])
            for h in range(HEADS):
                high, low = split(both[h])
                spread_hi[h, pl.ds(base, 16), lanes] = high
                spread_lo[h, pl.ds(base, 16), lanes] = low
            return carry

        lax.fori_loop(0, 32, put, 0)
        for h in range(HEADS):
            for i in range(te // 16):
                mixed = jnp.zeros((16, 128), f32)
                for k in range(neigh):
                    mixed += code[k, i * 16 : i * 16 + 16, lanes] * weights[h][k : k + 1, :]
                high, low = split(mixed)
                spread_hi[h, width + i * 16 : width + i * 16 + 16, lanes] = high
                spread_lo[h, width + i * 16 : width + i * 16 + 16, lanes] = low
        return carry

    lax.fori_loop(0, 4, attend, 0)
    att = []
    for h in range(HEADS):
        part = slice(h * 256, h * 256 + 256)
        value = jnp.concatenate([val_hi[part], value_t[part, width:]], axis=1)
        att.append(
            dot(value, spread_hi[h])
            + dot(value, spread_lo[h])
            + dot(val_lo[part], spread_hi[h, :width, :])
        )
    att = jnp.concatenate(att, axis=0).T.astype(bf16)
    loads[5].wait()
    emb[...] = (dst_mem + dot(att, w_out[...])).astype(bf16)
    emb_copy = pltpu.make_async_copy(emb, emb_hbm, emb_sem)
    emb_copy.start()
    loads[6].wait()
    hidden = (
        dot(src_mem, w_msg1[:width, :])
        + dot(emb[...], w_msg1[width : 2 * width, :])
        + dot(ev_code[...], w_msg1[2 * width :, :])
    )
    hidden = jnp.maximum(hidden, 0.0).astype(bf16)
    loads[7].wait()
    owns = []
    for half in range(2):
        part = slice(half * 512, half * 512 + 512)
        message = dot(hidden, w_msg2[:, part]).astype(bf16)
        sums = dot(dst_hot_t[...], message)
        for c in range(4):
            stage[pl.ds(c, 512, stride=4), :] = sums[:, c * 128 : (c + 1) * 128]
        part_out[half] = stage[...].astype(bf16).reshape(n, 16, 128)
        own = pltpu.make_async_copy(
            part_out.at[half, me], part_in.at[half, me], own_sem.at[3 + half]
        )
        own.start()
        owns.append(own)
        send_all(
            part_out.at[half], part_in.at[half], part_sem.at[2 * half], part_sem.at[2 * half + 1]
        )
    emb_copy.wait()
    loads[8].wait()
    for half in range(2):
        owns[half].wait()
        all_sent(
            part_out.at[half], part_in.at[half], part_sem.at[2 * half], part_sem.at[2 * half + 1]
        ).wait()
        stage[...] = part_in[half].reshape(n * 16, 128).astype(f32)
        for s in range(4):
            for c in range(4):
                partial[s * n : (s + 1) * n, c * 128 : (c + 1) * 128] = stage[
                    pl.ds(s * 4 + c, n, stride=16), :
                ].astype(bf16)
        total = dot(match_ref[...], partial[...])
        agg = jnp.concatenate(
            [total[:, c * 128 : (c + 1) * 128] * share[...] for c in range(4)], axis=1
        ).astype(bf16)
        gate = dot(agg, w_input[half * 512 : half * 512 + 512, :])
        if half == 0:
            gates[...] = gate
        else:
            gates[...] += gate

    def update_rows(i, carry):
        rows = pl.ds(pl.multiple_of(i * 64, 64), 64)
        reset = jax.nn.sigmoid(gates[rows, 0:width] + state[rows, 0:width])
        update = jax.nn.sigmoid(
            gates[rows, width : 2 * width] + state[rows, width : 2 * width]
        )
        new = jnp.tanh(gates[rows, 2 * width :] + reset * state[rows, 2 * width :])
        old = picked[rows, :].astype(f32)
        fresh_out[rows, :] = ((1.0 - update) * new + update * old).astype(bf16)
        return carry

    lax.fori_loop(0, 8, update_rows, 0)


def place_kernel(leader, fresh, memory, out):
    size = out.shape[0]
    base = pl.program_id(0) * size
    mask = (iota((size, 512), 0) + base) == leader[0:1, :]
    hit = jnp.max(jnp.where(mask, 1.0, 0.0), axis=1, keepdims=True)
    moved = dot(hot(mask), fresh[...])
    out[...] = jnp.where(hit > 0.0, moved, memory[...].astype(f32)).astype(bf16)


def per_device(
    memory,
    touched,
    src_pos,
    dst_owner,
    dst_slot,
    neighbors,
    ev_time,
    neigh_time,
    time_freq,
    w_query,
    w_key,
    w_value,
    w_out,
    w_msg1,
    w_msg2,
    w_input,
    w_hidden,
):
    owner = dst_owner[:, 0]
    dst_pos = owner * 4 + dst_slot
    ints = jnp.concatenate(
        [
            neighbors.T,
            (ev_time[:, None] - neigh_time).T,
            jnp.stack([src_pos, dst_pos, owner, dst_slot, ev_time, ev_time, ev_time, ev_time]),
        ],
        axis=0,
    )
    cols = jnp.stack([src_pos, dst_pos, ev_time], axis=1)
    asks = touched.reshape(16, 8, 4).transpose(1, 0, 2).reshape(128, 4)
    asks = jnp.pad(asks, ((0, 0), (0, 124)))
    vmem = pl.BlockSpec(memory_space=pltpu.VMEM)
    anyw = pl.BlockSpec(memory_space=pl.ANY)
    weights = (w_hidden, w_query, w_key, w_value, w_out, w_msg1, w_msg2, w_input)

    def local(*shape, dtype=bf16):
        return pltpu.VMEM(shape, dtype)

    sems = pltpu.SemaphoreType.DMA
    emb, fresh, leader = pl.pallas_call(
        window_kernel,
        out_shape=(
            jax.ShapeDtypeStruct((512, 512), bf16),
            jax.ShapeDtypeStruct((512, 512), bf16),
            jax.ShapeDtypeStruct((8, 512), i32),
        ),
        in_specs=[vmem] * 5 + [anyw] * 9,
        out_specs=(anyw, vmem, vmem),
        scratch_shapes=[
            local(*memory.shape),
            *[local(*w.shape) for w in weights],
            sems((9,)),
            sems,
            local(128, 128, dtype=i32),
            local(128, 128, dtype=i32),
            local(16, 8, 128, dtype=i32),
            local(16, 8, 128, dtype=i32),
            sems((4,)),
            sems((5,)),
            local(2048, 128, dtype=f32),
            local(128, 16, 128),
            local(128, 16, 128),
            sems((2,)),
            local(2, 128, 16, 128),
            local(2, 128, 16, 128),
            sems((4,)),
            local(16, 128, 512, dtype=f32),
            local(512, 512),
            local(512, 1536, dtype=f32),
            local(512, 640),
            local(512, 512),
            local(512, 128, dtype=f32),
            local(512, 128),
            local(512, 512),
            local(512, 512),
            local(512, 512),
            local(512, 512),
            local(2, 512, 512, dtype=f32),
            local(2, 128, 512, dtype=f32),
            local(2, 640, 512),
            local(2, 640, 512),
            local(512, 512),
            local(512, 512),
            local(512, 1536, dtype=f32),
        ],
        compiler_params=pltpu.CompilerParams(
            collective_id=0, has_side_effects=True, vmem_limit_bytes=60 << 20
        ),
        name="window",
    )(ints, cols, asks, time_freq[:, None], time_freq[None, :], memory, *weights)
    rows = 256
    new_memory = pl.pallas_call(
        place_kernel,
        grid=(memory.shape[0] // rows,),
        out_shape=jax.ShapeDtypeStruct(memory.shape, bf16),
        in_specs=[
            pl.BlockSpec((8, 512), lambda i: (0, 0)),
            pl.BlockSpec((512, 512), lambda i: (0, 0)),
            pl.BlockSpec((rows, 512), lambda i: (i, 0)),
        ],
        out_specs=pl.BlockSpec((rows, 512), lambda i: (i, 0)),
        compiler_params=pltpu.CompilerParams(vmem_limit_bytes=32 << 20),
        name="place",
    )(leader, fresh, memory)
    return emb, new_memory


def solution(mesh):
    rows = P(("owner", "group"))
    in_specs = (rows,) * 8 + (P(),) * 9
    return jax.shard_map(
        per_device, mesh=mesh, in_specs=in_specs, out_specs=(rows, rows), check_vma=False
    )
```

time: 174 us -> 81.2 us (0.47)
  matrix products: 55.7 us -> 0 us
  other arithmetic: 30 us -> 2.84 us
  local copies, waits for them, and re-layouts: 31.5 us -> 9.82 us
  Pallas kernels: 54.7 us -> 67.3 us
    dot_general x16 -> x0, matrix products: 55.7 us -> none  [the longest x12 31 us: dot(): return jnp.dot(a, b, preferred_element_type=jnp.float32)]
    convert_element_type x7 -> x0, other arithmetic: 18.8 us -> none  [the longest x2 15.9 us: time_code(): jnp.cos(delta.astype(jnp.float32)[..., None] * time_freq)]
    reshape x7 -> x1, local copies, waits for them, and re-layouts: 14.5 us -> 0.77 us  [per_device(): asks = touched.reshape(16, 8, 4).transpose(1, 0, 2).reshape(128, 4)]
    pallas_call x3 -> x2, Pallas kernels: 54.7 us -> 67.3 us  [the longest x1 62.9 us: per_device(): pl.pallas_call(window_kernel, out_shape=(jax.ShapeDtypeStruct((512, 512),...]
    eq x8 -> x0, other arithmetic: 8.94 us -> none  [per_device(): neighbors[:, k][:, None] == jnp.arange(positions, dtype=jnp.int32)[None, :]]
    dot_general x4 -> x0, local copies, waits for them, and re-layouts: 6.84 us -> none  [dot(): return jnp.dot(a, b, preferred_element_type=jnp.float32)]
    unnamed x77 -> x9, local copies, waits for them, and re-layouts: 7.75 us -> 2.55 us
    concatenate x1, local copies, waits for them, and re-layouts: 0.07 us -> 3.45 us  [per_device(): jnp.concatenate([neighbors.T, (ev_time[:, None] - neigh_time).T, jnp.stac...]
where the time goes in v1:
time: 81.2 us; the launch traced here: 80.7 us
  Pallas kernels  67.3 us (83%)
  local copies, waits for them, and re-layouts  9.82 us (12%)
  other arithmetic  2.84 us (3%)
    pallas_call x1, Pallas kernels, per_device(): pl.pallas_call(window_kernel, out_shape=(jax.ShapeDtypeStruct((512, 512),...  62.9 us
    pallas_call x1, Pallas kernels, per_device(): pl.pallas_call(place_kernel, grid=(memory.shape[0] // rows,), out_shape=j...  4.41 us
    concatenate x1, local copies, waits for them, and re-layouts, per_device(): jnp.concatenate([neighbors.T, (ev_time[:, None] - neigh_time).T, jnp.stac...  3.45 us
    unnamed x9, local copies, waits for them, and re-layouts  2.55 us

profile of v1, /device:TPU:1, one launch (start us, length us, event | category | flops | bytes accessed | tf_op | source)
XLA Modules:
  0.0 80.7 jit_solution(7357220215501757769)
XLA Ops:
  0.6 0.7 broadcast_multiply_fusion
  1.3 0.7 add.5
  2.0 0.7 pad_add_fusion
  2.7 0.8 reshape.13
  3.5 0.2 copy.26
  3.7 0.6 pad.4.asks
  4.3 0.8 subtract_bitcast_fusion
  5.1 3.4 %concatenate.3.ints = s32[40,512]{1,0:T(8,128)} concatenate(s32[16,512]{1,0:T(8,128)} %bitcast.25, s32[16,512]{1,0:T(8,128)S(1)} %subtract_bitcast_fusion, s32[1,512]{1,0:T(1,128)} %bitcast.29, s32[1,512]{1,0:T(1,128)S(1)} %bitcast.27, s32[1,512]{1,0:T(1,128)} %bitcast.31, s32[1,512]{1,0:T(1,128)} %bitcast.30, s32[1,512]{1,0:T(1,128)} %bitcast.21, s32[1,512]{1,0:T(1,128)} %bitcast.22, ...), dimensions={0} | concatenate | bytes 163840 | tf_op jit(solution)/shard_map/concatenate | solution.py:473
  8.5 1.4 %copy.28.freq_col = f32[128,1]{1,0:T(8,128)} copy(f32[128,1]{0,1:T(1,128)} %bitcast.33) | data formatting | bytes 1024 | tf_op jit(solution)/shard_map/broadcast_in_dim | solution.py:542
  9.9 0.9 %copy.27.cols = s32[512,3]{1,0:T(8,128)} copy(s32[512,3]{0,1:T(4,128)S(1)} %pad_add_fusion) | data formatting | bytes 12288 | tf_op jit(solution)/shard_map/stack | solution.py:481
  10.8 0.0 copy-start
  10.8 62.9 %window.1 = (bf16[512,512]{1,0:T(8,128)(2,1)}, bf16[512,512]{1,0:T(8,128)(2,1)}, s32[8,512]{1,0:T(8,128)}) custom-call(s32[40,512]{1,0:T(8,128)} %concatenate.3.ints, s32[512,3]{1,0:T(8,128)} %copy.27.cols, s32[128,128]{1,0:T(8,128)} %pad.4.asks, f32[128,1]{1,0:T(8,128)} %copy.28.freq_col, f32[1,128]{1,0:T(1,128)} %bitcast.34, bf16[2048,512]{1,0:T(8,128)(2,1)} %memory.1, ...), custom_call_target="tpu_custom_call" | custom-call | tf_op jit(solution)/shard_map/window/pallas_call | solution.py:492
  73.7 0.0 copy-done
  73.7 0.0 copy-start.1
  73.7 1.0 %copy-done.1 = bf16[512,512]{1,0:T(8,128)(2,1)S(1)} copy-done((bf16[512,512]{1,0:T(8,128)(2,1)S(1)}, bf16[512,512]{1,0:T(8,128)(2,1)}, u32[]{:S(2)}) %copy-start.1) | copy-done | bytes 524312
  74.7 0.0 copy-start.2
  74.8 0.7 copy-done.2
  75.5 0.0 copy-start.3
  75.5 4.4 %place.1 = bf16[2048,512]{1,0:T(8,128)(2,1)} custom-call(s32[8,512]{1,0:T(8,128)S(1)} %copy-done.2, bf16[512,512]{1,0:T(8,128)(2,1)S(1)} %copy-done.1, bf16[2048,512]{1,0:T(8,128)(2,1)S(1)} %copy-done), custom_call_target="tpu_custom_call" | custom-call | tf_op jit(solution)/shard_map/place/pallas_call | solution.py:544
  79.9 0.0 copy-done.3
  79.9 0.8 copy.30
Async XLA Ops:
  10.8 62.9 %copy-start = (bf16[2048,512]{1,0:T(8,128)(2,1)S(1)}, bf16[2048,512]{1,0:T(8,128)(2,1)}, u32[]{:S(2)}) copy-start(bf16[2048,512]{1,0:T(8,128)(2,1)} %memory.1) | copy-start | bytes 6291460
  73.7 1.0 %copy-start.1 = (bf16[512,512]{1,0:T(8,128)(2,1)S(1)}, bf16[512,512]{1,0:T(8,128)(2,1)}, u32[]{:S(2)}) copy-start(bf16[512,512]{1,0:T(8,128)(2,1)} %get-tuple-element.7.fresh) | copy-start | bytes 1572868
  74.7 0.7 copy-start.2
  75.5 4.4 %copy-start.3 = (bf16[512,512]{1,0:T(8,128)(2,1)S(1)}, bf16[512,512]{1,0:T(8,128)(2,1)}, u32[]{:S(2)}) copy-start(bf16[512,512]{1,0:T(8,128)(2,1)} %get-tuple-element.10) | copy-start | bytes 1572868

commit v2 on v1

--- a/solution.py
+++ b/solution.py
@@ -48,11 +48,14 @@
 
 
 def window_kernel(
-    ints,
-    cols,
-    asks,
-    freq_col,
-    freq_row,
+    touched,
+    src_pos,
+    dst_owner,
+    dst_slot,
+    neighbors,
+    ev_time,
+    neigh_time,
+    time_freq,
     memory_hbm,
     w_hidden_hbm,
     w_query_hbm,
@@ -63,8 +66,7 @@
     w_msg2_hbm,
     w_input_hbm,
     emb_hbm,
-    fresh_out,
-    leader_out,
+    new_hbm,
     memory,
     w_hidden,
     w_query,
@@ -76,6 +78,9 @@
     w_input,
     load_sem,
     emb_sem,
+    new_sem,
+    ints,
+    natural,
     note,
     note_in,
     relay,
@@ -107,6 +112,9 @@
     emb,
     partial,
     gates,
+    lead,
+    taken,
+    fresh,
 ):
     groups, owners = 8, 16
     n = groups * owners
@@ -141,11 +149,25 @@
         load.start()
         loads.append(load)
 
-    row = iota((n, 1), 0)
-    device = ((row & (owners - 1)) * groups) + (row // owners)
-    owner_hot = hot(device == ints[34:35, :])
-    slot_hot = hot(iota((n, 512), 0) == ints[35:36, :] + 4)
-    note[...] = asks[...] + dot(owner_hot, slot_hot, NT).astype(i32)
+    ints[0:neigh, :] = neighbors[...]
+    ints[neigh : 2 * neigh, :] = ev_time[...] - neigh_time[...]
+    ints[32:33, :] = src_pos[...]
+    ints[33:34, :] = dst_owner[...] * 4 + dst_slot[...]
+    ints[34:35, :] = ev_time[...]
+    ints[35:40, :] = jnp.zeros((5, 512), i32)
+    cols = ints[32:40, :].astype(f32).T.astype(i32)
+    freq_row = time_freq[...]
+    freq_col = jnp.broadcast_to(freq_row, (8, te)).T[:, 0:1]
+
+    owner_hot = hot(iota((n, 512), 0) == dst_owner[...])
+    slot_hot = hot(iota((n, 512), 0) == dst_slot[...] + 4)
+    natural[...] = dot(owner_hot, slot_hot, NT).astype(i32)
+    wanted = jnp.concatenate([touched[0], touched[0]], axis=0).astype(f32)
+    natural[:, 0:4] = wanted.T[:, 0:4].astype(i32)
+    for group in range(groups):
+        note[group * owners : (group + 1) * owners, :] = natural[
+            pl.ds(group, owners, stride=groups), :
+        ]
     pl.semaphore_wait(barrier, groups + owners - 2)
 
     def note_part(index):
@@ -165,15 +187,15 @@
         ).start()
 
     def make_codes(first):
-        def codes(i, carry):
-            rows = pl.ds(pl.multiple_of(i * 16, 16), 16)
-            freq = freq_col[rows, :]
-            for k in range(first, first + neigh // 2):
-                delta = ints[k + neigh : k + neigh + 1, :].astype(f32)
-                code[k, rows, :] = cosine(freq * delta).astype(bf16).astype(f32)
+        def codes(k, carry):
+            for i in range(te // 32):
+                rows = slice(i * 32, i * 32 + 32)
+                code[k, rows, :] = cosine(freq_col[rows] * delta).astype(bf16).astype(f32)
             return carry
 
-        lax.fori_loop(0, te // 16, codes, 0)
+        for k in range(first, first + neigh // 2):
+            delta = ints[k + neigh : k + neigh + 1, :].astype(f32)
+            codes(k, 0)
 
     make_codes(0)
     own.wait()
@@ -266,8 +288,13 @@
     earlier = match & (iota((512, 512), 0) < iota((512, 512), 1))
     earlier = jnp.sum(jnp.where(earlier, 1.0, 0.0), axis=0, keepdims=True)
     leader = jnp.where((earlier == 0.0) & (number_row > 0.0), asked_row, -1)
-    leader_out[...] = jnp.broadcast_to(leader, leader_out.shape)
-    ev_code[...] = cosine(cols[:, 2:3].astype(f32) * freq_row[...]).astype(bf16)
+    for i in range(8):
+        rows = slice(i * 256, i * 256 + 256)
+        mask = (iota((256, 512), 0) + i * 256) == leader
+        lead[rows, :] = hot(mask)
+        hit = jnp.max(jnp.where(mask, 1.0, 0.0), axis=1, keepdims=True)
+        taken[rows, :] = jnp.broadcast_to(hit, (256, 128))
+    ev_code[...] = cosine(cols[:, 2:3].astype(f32) * freq_row).astype(bf16)
     src_hot[...] = hot(iota((512, 512), 1) == cols[:, 0:1])
     dst_hot[...] = hot(iota((512, 512), 1) == cols[:, 1:2])
     dst_hot_t[...] = hot(iota((512, 512), 0) == ints[33:34, :])
@@ -434,19 +461,24 @@
         )
         new = jnp.tanh(gates[rows, 2 * width :] + reset * state[rows, 2 * width :])
         old = picked[rows, :].astype(f32)
-        fresh_out[rows, :] = ((1.0 - update) * new + update * old).astype(bf16)
+        fresh[rows, :] = ((1.0 - update) * new + update * old).astype(bf16)
         return carry
 
     lax.fori_loop(0, 8, update_rows, 0)
 
-
-def place_kernel(leader, fresh, memory, out):
-    size = out.shape[0]
-    base = pl.program_id(0) * size
-    mask = (iota((size, 512), 0) + base) == leader[0:1, :]
-    hit = jnp.max(jnp.where(mask, 1.0, 0.0), axis=1, keepdims=True)
-    moved = dot(hot(mask), fresh[...])
-    out[...] = jnp.where(hit > 0.0, moved, memory[...].astype(f32)).astype(bf16)
+    def place(i, carry):
+        rows = pl.ds(pl.multiple_of(i * 256, 256), 256)
+        moved = dot(lead[rows, :], fresh[...])
+        mask = taken[rows, :] > 0.0
+        for c in range(4):
+            lanes = slice(c * 128, c * 128 + 128)
+            old = memory[rows, lanes].astype(f32)
+            memory[rows, lanes] = jnp.where(mask, moved[:, lanes], old).astype(bf16)
+        pltpu.make_async_copy(memory.at[rows], new_hbm.at[rows], new_sem).start()
+        return carry
+
+    lax.fori_loop(0, 8, place, 0)
+    pltpu.make_async_copy(memory, new_hbm, new_sem).wait()
 
 
 def per_device(
@@ -468,19 +500,6 @@
     w_input,
     w_hidden,
 ):
-    owner = dst_owner[:, 0]
-    dst_pos = owner * 4 + dst_slot
-    ints = jnp.concatenate(
-        [
-            neighbors.T,
-            (ev_time[:, None] - neigh_time).T,
-            jnp.stack([src_pos, dst_pos, owner, dst_slot, ev_time, ev_time, ev_time, ev_time]),
-        ],
-        axis=0,
-    )
-    cols = jnp.stack([src_pos, dst_pos, ev_time], axis=1)
-    asks = touched.reshape(16, 8, 4).transpose(1, 0, 2).reshape(128, 4)
-    asks = jnp.pad(asks, ((0, 0), (0, 124)))
     vmem = pl.BlockSpec(memory_space=pltpu.VMEM)
     anyw = pl.BlockSpec(memory_space=pl.ANY)
     weights = (w_hidden, w_query, w_key, w_value, w_out, w_msg1, w_msg2, w_input)
@@ -489,20 +508,22 @@
         return pltpu.VMEM(shape, dtype)
 
     sems = pltpu.SemaphoreType.DMA
-    emb, fresh, leader = pl.pallas_call(
+    return pl.pallas_call(
         window_kernel,
         out_shape=(
             jax.ShapeDtypeStruct((512, 512), bf16),
-            jax.ShapeDtypeStruct((512, 512), bf16),
-            jax.ShapeDtypeStruct((8, 512), i32),
+            jax.ShapeDtypeStruct(memory.shape, bf16),
         ),
-        in_specs=[vmem] * 5 + [anyw] * 9,
-        out_specs=(anyw, vmem, vmem),
+        in_specs=[vmem] * 8 + [anyw] * 9,
+        out_specs=(anyw, anyw),
         scratch_shapes=[
             local(*memory.shape),
             *[local(*w.shape) for w in weights],
             sems((9,)),
             sems,
+            sems,
+            local(40, 512, dtype=i32),
+            local(128, 128, dtype=i32),
             local(128, 128, dtype=i32),
             local(128, 128, dtype=i32),
             local(16, 8, 128, dtype=i32),
@@ -534,27 +555,26 @@
             local(512, 512),
             local(512, 512),
             local(512, 1536, dtype=f32),
+            local(*memory.shape),
+            local(memory.shape[0], 128, dtype=f32),
+            local(512, 512),
         ],
         compiler_params=pltpu.CompilerParams(
             collective_id=0, has_side_effects=True, vmem_limit_bytes=60 << 20
         ),
         name="window",
-    )(ints, cols, asks, time_freq[:, None], time_freq[None, :], memory, *weights)
-    rows = 256
-    new_memory = pl.pallas_call(
-        place_kernel,
-        grid=(memory.shape[0] // rows,),
-        out_shape=jax.ShapeDtypeStruct(memory.shape, bf16),
-        in_specs=[
-            pl.BlockSpec((8, 512), lambda i: (0, 0)),
-            pl.BlockSpec((512, 512), lambda i: (0, 0)),
-            pl.BlockSpec((rows, 512), lambda i: (i, 0)),
-        ],
-        out_specs=pl.BlockSpec((rows, 512), lambda i: (i, 0)),
-        compiler_params=pltpu.CompilerParams(vmem_limit_bytes=32 << 20),
-        name="place",
-    )(leader, fresh, memory)
-    return emb, new_memory
+    )(
+        touched.transpose(0, 2, 1),
+        src_pos[None, :],
+        dst_owner.reshape(1, -1),
+        dst_slot[None, :],
+        neighbors.T,
+        ev_time[None, :],
+        neigh_time.T,
+        time_freq[None, :],
+        memory,
+        *weights,
+    )
 
 
 def solution(mesh):

time: 81.2 us -> 70.9 us (0.87)
  local copies, waits for them, and re-layouts: 9.82 us -> 4.91 us
  other arithmetic: 2.84 us -> 0 us
  Pallas kernels: 67.3 us -> 65.1 us
    pallas_call x1 -> x0, Pallas kernels: 4.41 us -> none  [per_device(): pl.pallas_call(place_kernel, grid=(memory.shape[0] // rows,), out_shape=j...]
    concatenate x1 -> x0, local copies, waits for them, and re-layouts: 3.45 us -> none  [per_device(): jnp.concatenate([neighbors.T, (ev_time[:, None] - neigh_time).T, jnp.stac...]
    unnamed x9 -> x2, local copies, waits for them, and re-layouts: 2.55 us -> 4.91 us
    pallas_call x1, Pallas kernels: 62.9 us -> 65.1 us  [per_device(): pl.pallas_call(window_kernel, out_shape=(jax.ShapeDtypeStruct((512, 512),...]
    broadcast_in_dim x1 -> x0, local copies, waits for them, and re-layouts: 1.38 us -> none  [per_device(): time_freq[:, None]]
    another operation x1 -> x0, local copies, waits for them, and re-layouts: 0.86 us -> none  [per_device(): cols = jnp.stack([src_pos, dst_pos, ev_time], axis=1)]
where the time goes in v2:
time: 70.9 us; the launch traced here: 70.7 us
  Pallas kernels  65.1 us (92%)
  local copies, waits for them, and re-layouts  4.91 us (7%)
    pallas_call x1, Pallas kernels, per_device(): pl.pallas_call(window_kernel, out_shape=(jax.ShapeDtypeStruct((512, 512),...  65.1 us
    unnamed x2, local copies, waits for them, and re-layouts  4.91 us

profile of v2, /device:TPU:1, one launch (start us, length us, event | category | flops | bytes accessed | tf_op | source)
XLA Modules:
  0.0 70.7 jit_solution(3072759104521604861)
XLA Ops:
  0.6 65.1 %window.1 = (bf16[512,512]{1,0:T(8,128)(2,1)}, bf16[2048,512]{1,0:T(8,128)(2,1)}) custom-call(s32[1,4,128]{2,1,0:T(4,128)} %bitcast.10, s32[1,512]{1,0:T(1,128)} %bitcast.11, s32[1,512]{1,0:T(1,128)} %bitcast.12, s32[1,512]{1,0:T(1,128)} %bitcast.13, s32[16,512]{1,0:T(8,128)} %bitcast.8, s32[1,512]{1,0:T(1,128)} %bitcast.14, s32[16,512]{1,0:T(8,128)} %bitcast.9, ...), custom_call_target="tpu_custom_call" | custom-call | tf_op jit(solution)/shard_map/window/pallas_call | solution.py:511
  65.8 1.9 %copy.21 = bf16[512,512]{1,0:T(8,128)(2,1)} copy(bf16[512,512]{1,0:T(8,128)(2,1)} %get-tuple-element.4) | data formatting | bytes 1048576
  67.6 3.0 %copy.22 = bf16[2048,512]{1,0:T(8,128)(2,1)} copy(bf16[2048,512]{1,0:T(8,128)(2,1)} %get-tuple-element.5) | data formatting | bytes 4194304

commit v3 on v2

--- a/solution.py
+++ b/solution.py
@@ -35,6 +35,10 @@
 def split(x):
     high = x.astype(bf16)
     return high, (x - high.astype(f32)).astype(bf16)
+
+
+def take(x, index):
+    return jnp.take_along_axis(x, index, axis=0, mode="promise_in_bounds")
 
 
 def cosine(x):
@@ -66,7 +70,8 @@
     w_msg2_hbm,
     w_input_hbm,
     emb_hbm,
-    new_hbm,
+    fresh_hbm,
+    lead_hbm,
     memory,
     w_hidden,
     w_query,
@@ -82,8 +87,6 @@
     ints,
     natural,
     note,
-    note_in,
-    relay,
     notes,
     note_sem,
     own_sem,
@@ -113,8 +116,9 @@
     partial,
     gates,
     lead,
-    taken,
+    lead_sem,
     fresh,
+    finder,
 ):
     groups, owners = 8, 16
     n = groups * owners
@@ -123,14 +127,18 @@
     neigh, te, width = 16, 128, 512
 
     barrier = pltpu.get_barrier_semaphore()
-    for step in range(1, groups):
+
+    def greet(step, carry):
+        peer = (me + step) & (n - 1)
         pl.semaphore_signal(
-            barrier, inc=1, device_id=(o, (g + step) & (groups - 1)), device_id_type=MESH
-        )
-    for step in range(1, owners):
-        pl.semaphore_signal(
-            barrier, inc=1, device_id=((o + step) & (owners - 1), g), device_id_type=MESH
-        )
+            barrier,
+            inc=1,
+            device_id=(peer // groups, peer & (groups - 1)),
+            device_id_type=MESH,
+        )
+        return carry
+
+    lax.fori_loop(1, n, greet, 0)
     loads = []
     for number, (source, target) in enumerate(
         (
@@ -164,84 +172,8 @@
     natural[...] = dot(owner_hot, slot_hot, NT).astype(i32)
     wanted = jnp.concatenate([touched[0], touched[0]], axis=0).astype(f32)
     natural[:, 0:4] = wanted.T[:, 0:4].astype(i32)
-    for group in range(groups):
-        note[group * owners : (group + 1) * owners, :] = natural[
-            pl.ds(group, owners, stride=groups), :
-        ]
-    pl.semaphore_wait(barrier, groups + owners - 2)
-
-    def note_part(index):
-        return pl.ds(pl.multiple_of(index * owners, owners), owners)
-
-    own = pltpu.make_async_copy(note.at[note_part(g)], note_in.at[note_part(g)], own_sem.at[0])
-    own.start()
-    for step in range(1, groups):
-        peer = (g + step) & (groups - 1)
-        pltpu.make_async_remote_copy(
-            src_ref=note.at[note_part(peer)],
-            dst_ref=note_in.at[note_part(g)],
-            send_sem=note_sem.at[0],
-            recv_sem=note_sem.at[1],
-            device_id=(o, peer),
-            device_id_type=MESH,
-        ).start()
-
-    def make_codes(first):
-        def codes(k, carry):
-            for i in range(te // 32):
-                rows = slice(i * 32, i * 32 + 32)
-                code[k, rows, :] = cosine(freq_col[rows] * delta).astype(bf16).astype(f32)
-            return carry
-
-        for k in range(first, first + neigh // 2):
-            delta = ints[k + neigh : k + neigh + 1, :].astype(f32)
-            codes(k, 0)
-
-    make_codes(0)
-    own.wait()
-    some = (groups - 1) * owners
-    pltpu.make_async_remote_copy(
-        src_ref=note.at[pl.ds(0, some)],
-        dst_ref=note_in.at[pl.ds(0, some)],
-        send_sem=note_sem.at[0],
-        recv_sem=note_sem.at[1],
-        device_id=(o, (g + 1) & (groups - 1)),
-        device_id_type=MESH,
-    ).wait()
-    for owner in range(owners):
-        relay[owner] = note_in[pl.ds(owner, groups, stride=owners), :]
-    own = pltpu.make_async_copy(relay.at[o], notes.at[o], own_sem.at[1])
-    own.start()
-    for step in range(1, owners):
-        peer = (o + step) & (owners - 1)
-        pltpu.make_async_remote_copy(
-            src_ref=relay.at[peer],
-            dst_ref=notes.at[o],
-            send_sem=note_sem.at[2],
-            recv_sem=note_sem.at[3],
-            device_id=(peer, g),
-            device_id_type=MESH,
-        ).start()
-    make_codes(neigh // 2)
-    own.wait()
-    pltpu.make_async_remote_copy(
-        src_ref=relay.at[pl.ds(0, owners - 1)],
-        dst_ref=notes.at[pl.ds(0, owners - 1)],
-        send_sem=note_sem.at[2],
-        recv_sem=note_sem.at[3],
-        device_id=((o + 1) & (owners - 1), g),
-        device_id_type=MESH,
-    ).wait()
-    known = notes[...].reshape(n, 128)
-    known_t = known.astype(f32).T.astype(i32)
-
-    loads[0].wait()
-    for s in range(4):
-        rows = dot(hot(iota((n, 2048), 1) == known[:, s : s + 1]), memory[...])
-        picked[s * n : (s + 1) * n, :] = rows.astype(bf16)
-        for c in range(4):
-            stage[pl.ds(s * 4 + c, n, stride=16), :] = rows[:, c * 128 : (c + 1) * 128]
-    outbox[...] = stage[...].astype(bf16).reshape(n, 16, 128)
+    note[:, 0, :] = natural[...]
+    pl.semaphore_wait(barrier, n - 1)
 
     def send_all(source, target, send_sem, recv_sem):
         def send(step, carry):
@@ -267,6 +199,56 @@
             device_id=(o, (g + 1) & (groups - 1)),
             device_id_type=MESH,
         )
+
+    own = pltpu.make_async_copy(note.at[me], notes.at[me], own_sem.at[0])
+    own.start()
+    send_all(note, notes, note_sem.at[0], note_sem.at[1])
+
+    def make_codes(first):
+        def codes(k, carry):
+            for i in range(te // 32):
+                rows = slice(i * 32, i * 32 + 32)
+                code[k, rows, :] = cosine(freq_col[rows] * delta).astype(bf16).astype(f32)
+            return carry
+
+        for k in range(first, first + neigh // 2):
+            delta = ints[k + neigh : k + neigh + 1, :].astype(f32)
+            codes(k, 0)
+
+    make_codes(0)
+    make_codes(neigh // 2)
+
+    def find(piece, carry):
+        lanes = pl.ds(pl.multiple_of(piece * 128, 128), 128)
+        near = ints[0:neigh, lanes]
+        near8 = [jnp.broadcast_to(near[k : k + 1, :], (8, 128)) for k in range(neigh)]
+        sub = iota((8, 128), 0)
+
+        def scan(i, carry):
+            for u in range(4):
+                base = pl.multiple_of(i * 32 + u * 8, 8)
+                which = jnp.full((8, 128), neigh, i32)
+                for k in range(neigh):
+                    which = jnp.where(sub + base == near8[k], k, which)
+                finder[pl.ds(base, 8), lanes] = which
+            return carry
+
+        lax.fori_loop(0, 16, scan, 0)
+        return carry
+
+    lax.fori_loop(0, 4, find, 0)
+    own.wait()
+    all_sent(note, notes, note_sem.at[0], note_sem.at[1]).wait()
+    known = notes[:, 0, :]
+    known_t = known.astype(f32).T.astype(i32)
+
+    loads[0].wait()
+    for s in range(4):
+        rows = dot(hot(iota((n, 2048), 1) == known[:, s : s + 1]), memory[...])
+        picked[s * n : (s + 1) * n, :] = rows.astype(bf16)
+        for c in range(4):
+            stage[pl.ds(s * 4 + c, n, stride=16), :] = rows[:, c * 128 : (c + 1) * 128]
+    outbox[...] = stage[...].astype(bf16).reshape(n, 16, 128)
 
     own = pltpu.make_async_copy(outbox.at[me], inbox.at[me], own_sem.at[2])
     own.start()
@@ -288,12 +270,9 @@
     earlier = match & (iota((512, 512), 0) < iota((512, 512), 1))
     earlier = jnp.sum(jnp.where(earlier, 1.0, 0.0), axis=0, keepdims=True)
     leader = jnp.where((earlier == 0.0) & (number_row > 0.0), asked_row, -1)
-    for i in range(8):
-        rows = slice(i * 256, i * 256 + 256)
-        mask = (iota((256, 512), 0) + i * 256) == leader
-        lead[rows, :] = hot(mask)
-        hit = jnp.max(jnp.where(mask, 1.0, 0.0), axis=1, keepdims=True)
-        taken[rows, :] = jnp.broadcast_to(hit, (256, 128))
+    lead[...] = jnp.broadcast_to(leader, lead.shape)
+    lead_copy = pltpu.make_async_copy(lead, lead_hbm, lead_sem)
+    lead_copy.start()
     ev_code[...] = cosine(cols[:, 2:3].astype(f32) * freq_row).astype(bf16)
     src_hot[...] = hot(iota((512, 512), 1) == cols[:, 0:1])
     dst_hot[...] = hot(iota((512, 512), 1) == cols[:, 1:2])
@@ -327,68 +306,95 @@
     def attend(piece, carry):
         lanes = pl.ds(pl.multiple_of(piece * 128, 128), 128)
         near = ints[0:neigh, lanes]
-        near8 = [jnp.broadcast_to(near[k : k + 1, :], (8, 128)) for k in range(neigh)]
-        sub = iota((8, 128), 0)
-
-        def look(i, sums):
+        fine = [near[b * 8 : b * 8 + 8, :] & 7 for b in range(2)]
+        coarse = [near[b * 8 : b * 8 + 8, :] >> 3 for b in range(2)]
+
+        def look(i, found):
+            found = list(found)
+            for u in range(8):
+                base = pl.multiple_of(i * 64 + u * 8, 8)
+                for b in range(2):
+                    mask = coarse[b] == i * 8 + u
+                    for h in range(HEADS):
+                        taken = take(full[h, pl.ds(base, 8), lanes], fine[b])
+                        found[h * 2 + b] = jnp.where(mask, taken, found[h * 2 + b])
+            return tuple(found)
+
+        zero = jnp.zeros((8, 128), f32)
+        found = lax.fori_loop(0, 8, look, (zero,) * (2 * HEADS))
+
+        def timed(i, sums):
             sums = list(sums)
-            for u in range(4):
-                base = pl.multiple_of(i * 32 + u * 8, 8)
-                place = sub + base
-                first = full[0, pl.ds(base, 8), lanes]
-                second = full[1, pl.ds(base, 8), lanes]
-                for k in range(neigh):
-                    mask = place == near8[k]
-                    sums[k] = jnp.where(mask, first, sums[k])
-                    sums[neigh + k] = jnp.where(mask, second, sums[neigh + k])
+            rows = pl.ds(pl.multiple_of(i * 8, 8), 8)
+            mine = [query_code[h, rows, lanes] for h in range(HEADS)]
+            for k in range(neigh):
+                one = code[k, rows, lanes]
+                for h in range(HEADS):
+                    sums[h * neigh + k] += one * mine[h]
             return tuple(sums)
 
-        zero = jnp.zeros((8, 128), f32)
-        sums = list(lax.fori_loop(0, 16, look, (zero,) * (2 * neigh)))
-        rows = [[], []]
-        for h in range(HEADS):
-            mine = query_code[h, :, lanes]
-            for k in range(neigh):
-                prod = (code[k, :, lanes] * mine).reshape(te // 8, 8, 128)
-                prod = jnp.sum(prod, axis=0) + sums[h * neigh + k]
-                rows[h].append(jnp.sum(prod, axis=0, keepdims=True))
+        sums = lax.fori_loop(0, te // 8, timed, (zero,) * (HEADS * neigh))
         whole = []
         weights = []
         for h in range(HEADS):
-            score = jnp.concatenate(rows[h], axis=0)
+            score = jnp.concatenate(
+                [
+                    jnp.sum(sums[h * neigh + k], axis=0, keepdims=True)
+                    for k in range(neigh)
+                ],
+                axis=0,
+            ) + jnp.concatenate(found[h * 2 : h * 2 + 2], axis=0)
             score = jnp.exp(score - jnp.max(score, axis=0, keepdims=True))
             weight = score / jnp.sum(score, axis=0, keepdims=True)
             total = jnp.zeros((neigh, 128), f32)
             for k in range(neigh):
                 total += jnp.where(near == near[k : k + 1, :], weight[k : k + 1, :], 0.0)
             weights.append(weight)
-            whole.append([jnp.broadcast_to(total[k : k + 1, :], (16, 128)) for k in range(neigh)])
-        near16 = [jnp.broadcast_to(near[k : k + 1, :], (16, 128)) for k in range(neigh)]
-        sub16 = iota((16, 128), 0)
+            whole.append([total[0:8, :], total[8:16, :]])
 
         def put(i, carry):
+            for u in range(4):
+                base = pl.multiple_of(i * 64 + u * 16, 16)
+                both = [[], []]
+                for v in range(2):
+                    which = finder[pl.ds(base + v * 8, 8), lanes]
+                    fine = which & 7
+                    for h in range(HEADS):
+                        first = jnp.where(which < 8, take(whole[h][0], fine), 0.0)
+                        second = take(whole[h][1], fine)
+                        both[h].append(
+                            jnp.where((which & 24) == 8, second, first)
+                        )
+                for h in range(HEADS):
+                    high, low = split(jnp.concatenate(both[h], axis=0))
+                    spread_hi[h, pl.ds(base, 16), lanes] = high
+                    spread_lo[h, pl.ds(base, 16), lanes] = low
+            return carry
+
+        lax.fori_loop(0, 8, put, 0)
+        spread = [
+            [jnp.broadcast_to(weights[h][k : k + 1, :], (8, 128)) for k in range(neigh)]
+            for h in range(HEADS)
+        ]
+
+        def mix(i, carry):
             base = pl.multiple_of(i * 16, 16)
-            place = sub16 + base
-            both = [jnp.zeros((16, 128), f32)] * HEADS
-            for k in range(neigh):
-                mask = place == near16[k]
+            both = [[], []]
+            for v in range(2):
+                mixed = [zero] * HEADS
+                for k in range(neigh):
+                    one = code[k, pl.ds(base + v * 8, 8), lanes]
+                    for h in range(HEADS):
+                        mixed[h] += one * spread[h][k]
                 for h in range(HEADS):
-                    both[h] = jnp.where(mask, whole[h][k], both[h])
+                    both[h].append(mixed[h])
             for h in range(HEADS):
-                high, low = split(both[h])
-                spread_hi[h, pl.ds(base, 16), lanes] = high
-                spread_lo[h, pl.ds(base, 16), lanes] = low
+                high, low = split(jnp.concatenate(both[h], axis=0))
+                spread_hi[h, pl.ds(width + base, 16), lanes] = high
+                spread_lo[h, pl.ds(width + base, 16), lanes] = low
             return carry
 
-        lax.fori_loop(0, 32, put, 0)
-        for h in range(HEADS):
-            for i in range(te // 16):
-                mixed = jnp.zeros((16, 128), f32)
-                for k in range(neigh):
-                    mixed += code[k, i * 16 : i * 16 + 16, lanes] * weights[h][k : k + 1, :]
-                high, low = split(mixed)
-                spread_hi[h, width + i * 16 : width + i * 16 + 16, lanes] = high
-                spread_lo[h, width + i * 16 : width + i * 16 + 16, lanes] = low
+        lax.fori_loop(0, te // 16, mix, 0)
         return carry
 
     lax.fori_loop(0, 4, attend, 0)
@@ -466,19 +472,57 @@
 
     lax.fori_loop(0, 8, update_rows, 0)
 
-    def place(i, carry):
-        rows = pl.ds(pl.multiple_of(i * 256, 256), 256)
-        moved = dot(lead[rows, :], fresh[...])
-        mask = taken[rows, :] > 0.0
-        for c in range(4):
-            lanes = slice(c * 128, c * 128 + 128)
-            old = memory[rows, lanes].astype(f32)
-            memory[rows, lanes] = jnp.where(mask, moved[:, lanes], old).astype(bf16)
-        pltpu.make_async_copy(memory.at[rows], new_hbm.at[rows], new_sem).start()
-        return carry
-
-    lax.fori_loop(0, 8, place, 0)
-    pltpu.make_async_copy(memory, new_hbm, new_sem).wait()
+    fresh_copy = pltpu.make_async_copy(fresh, fresh_hbm, new_sem)
+    fresh_copy.start()
+    lead_copy.wait()
+    fresh_copy.wait()
+
+
+def place_kernel(
+    leader_hbm,
+    fresh_hbm,
+    memory_hbm,
+    emb_hbm,
+    emb_out,
+    new_hbm,
+    leader,
+    fresh,
+    memory,
+    moved,
+    sem,
+    in_sem,
+    out_sem,
+):
+    emb_copy = pltpu.make_async_copy(emb_hbm, emb_out, sem.at[0])
+    emb_copy.start()
+    leader_copy = pltpu.make_async_copy(leader_hbm, leader, sem.at[1])
+    leader_copy.start()
+    fresh_copy = pltpu.make_async_copy(fresh_hbm, fresh, sem.at[2])
+    fresh_copy.start()
+    blocks = []
+    for i in range(8):
+        rows = pl.ds(i * 256, 256)
+        block = pltpu.make_async_copy(memory_hbm.at[rows], memory.at[rows], in_sem.at[i])
+        block.start()
+        blocks.append(block)
+    leader_copy.wait()
+    outs = []
+    for i in range(8):
+        rows = slice(i * 256, i * 256 + 256)
+        mask = iota((256, 512), 0) + i * 256 == leader[0:1, :]
+        hit = jnp.max(jnp.where(mask, 1.0, 0.0), axis=1, keepdims=True)
+        if i == 0:
+            fresh_copy.wait()
+        new = dot(hot(mask), fresh[...])
+        blocks[i].wait()
+        moved[rows, :] = jnp.where(hit > 0.0, new, memory[rows, :].astype(f32)).astype(bf16)
+        rows = pl.ds(i * 256, 256)
+        out = pltpu.make_async_copy(moved.at[rows], new_hbm.at[rows], out_sem.at[i])
+        out.start()
+        outs.append(out)
+    emb_copy.wait()
+    for out in outs:
+        out.wait()
 
 
 def per_device(
@@ -508,14 +552,15 @@
         return pltpu.VMEM(shape, dtype)
 
     sems = pltpu.SemaphoreType.DMA
-    return pl.pallas_call(
+    emb, fresh, leader = pl.pallas_call(
         window_kernel,
         out_shape=(
             jax.ShapeDtypeStruct((512, 512), bf16),
-            jax.ShapeDtypeStruct(memory.shape, bf16),
+            jax.ShapeDtypeStruct((512, 512), bf16),
+            jax.ShapeDtypeStruct((8, 512), i32),
         ),
         in_specs=[vmem] * 8 + [anyw] * 9,
-        out_specs=(anyw, anyw),
+        out_specs=(anyw,) * 3,
         scratch_shapes=[
             local(*memory.shape),
             *[local(*w.shape) for w in weights],
@@ -524,11 +569,9 @@
             sems,
             local(40, 512, dtype=i32),
             local(128, 128, dtype=i32),
-            local(128, 128, dtype=i32),
-            local(128, 128, dtype=i32),
-            local(16, 8, 128, dtype=i32),
-            local(16, 8, 128, dtype=i32),
-            sems((4,)),
+            local(128, 1, 128, dtype=i32),
+            local(128, 1, 128, dtype=i32),
+            sems((2,)),
             sems((5,)),
             local(2048, 128, dtype=f32),
             local(128, 16, 128),
@@ -555,9 +598,10 @@
             local(512, 512),
             local(512, 512),
             local(512, 1536, dtype=f32),
-            local(*memory.shape),
-            local(memory.shape[0], 128, dtype=f32),
-            local(512, 512),
+            local(8, 512, dtype=i32),
+            sems,
+            local(512, 512),
+            local(512, 512, dtype=i32),
         ],
         compiler_params=pltpu.CompilerParams(
             collective_id=0, has_side_effects=True, vmem_limit_bytes=60 << 20
@@ -575,6 +619,26 @@
         memory,
         *weights,
     )
+    return pl.pallas_call(
+        place_kernel,
+        out_shape=(
+            jax.ShapeDtypeStruct(emb.shape, bf16),
+            jax.ShapeDtypeStruct(memory.shape, bf16),
+        ),
+        in_specs=[anyw] * 4,
+        out_specs=(anyw, anyw),
+        scratch_shapes=[
+            local(8, 512, dtype=i32),
+            local(512, 512),
+            local(*memory.shape),
+            local(*memory.shape),
+            sems((3,)),
+            sems((8,)),
+            sems((8,)),
+        ],
+        compiler_params=pltpu.CompilerParams(vmem_limit_bytes=60 << 20),
+        name="place",
+    )(leader, fresh, memory, emb)
 
 
 def solution(mesh):

time: 70.9 us -> 77.4 us (1.092)
  Pallas kernels: 65.1 us -> 76.4 us
  local copies, waits for them, and re-layouts: 4.91 us -> 0 us
    pallas_call x0 -> x1, Pallas kernels: none -> 17.2 us  [per_device(): pl.pallas_call(place_kernel, out_shape=(jax.ShapeDtypeStruct(emb.shape, b...]
    pallas_call x1, Pallas kernels: 65.1 us -> 59.2 us  [per_device(): pl.pallas_call(window_kernel, out_shape=(jax.ShapeDtypeStruct((512, 512),...]
    unnamed x2 -> x0, local copies, waits for them, and re-layouts: 4.91 us -> none
where the time goes in v3:
time: 77.4 us; the launch traced here: 77.2 us
  Pallas kernels  76.4 us (99%)
  between operations  0.81 us (1%)
    pallas_call x1, Pallas kernels, per_device(): pl.pallas_call(window_kernel, out_shape=(jax.ShapeDtypeStruct((512, 512),...  59.2 us
    pallas_call x1, Pallas kernels, per_device(): pl.pallas_call(place_kernel, out_shape=(jax.ShapeDtypeStruct(emb.shape, b...  17.2 us

profile of v3, /device:TPU:1, one launch (start us, length us, event | category | flops | bytes accessed | tf_op | source)
XLA Modules:
  0.0 77.2 jit_solution(12206170453752511803)
XLA Ops:
  0.6 59.2 %window.1 = (bf16[512,512]{1,0:T(8,128)(2,1)}, bf16[512,512]{1,0:T(8,128)(2,1)}, s32[8,512]{1,0:T(8,128)}) custom-call(s32[1,4,128]{2,1,0:T(4,128)} %bitcast.10, s32[1,512]{1,0:T(1,128)} %bitcast.11, s32[1,512]{1,0:T(1,128)} %bitcast.12, s32[1,512]{1,0:T(1,128)} %bitcast.13, s32[16,512]{1,0:T(8,128)} %bitcast.8, s32[1,512]{1,0:T(1,128)} %bitcast.14, ...), custom_call_target="tpu_custom_call" | custom-call | tf_op jit(solution)/shard_map/window/pallas_call | solution.py:555
  59.8 17.2 %place.1 = (bf16[512,512]{1,0:T(8,128)(2,1)}, bf16[2048,512]{1,0:T(8,128)(2,1)}) custom-call(s32[8,512]{1,0:T(8,128)} %get-tuple-element.5.leader_hbm, bf16[512,512]{1,0:T(8,128)(2,1)} %get-tuple-element.6.fresh_hbm, bf16[2048,512]{1,0:T(8,128)(2,1)} %memory_hbm.3, bf16[512,512]{1,0:T(8,128)(2,1)} %get-tuple-element.7.emb_hbm), custom_call_target="tpu_custom_call" | custom-call | tf_op jit(solution)/shard_map/place/pallas_call | solution.py:622

commit v4 on v3

--- a/solution.py
+++ b/solution.py
@@ -119,6 +119,13 @@
     lead_sem,
     fresh,
     finder,
+    query_hi,
+    query_lo,
+    key_hi,
+    key_lo,
+    value_hi,
+    value_lo,
+    before,
 ):
     groups, owners = 8, 16
     n = groups * owners
@@ -258,6 +265,7 @@
     state[...] = dot(picked[...], w_hidden[...])
     loads[2].wait()
     value_t[...] = w_value[...].astype(f32).T.astype(bf16)
+    value_hi[:, width:] = value_t[:, width:]
     asked_col = jnp.concatenate([known[:, s : s + 1] for s in range(4)], axis=0)
     count_col = jnp.concatenate([known[:, s + 4 : s + 5] for s in range(4)], axis=0)
     asked_row = jnp.concatenate([known_t[s : s + 1, :] for s in range(4)], axis=1)
@@ -285,30 +293,48 @@
         table[:, c * 128 : (c + 1) * 128] = stage[pl.ds(c, 512, stride=4), :].astype(bf16)
 
     dst_mem = dot(dst_hot[...], table[...])
-    src_mem = dot(src_hot[...], table[...]).astype(bf16)
     loads[3].wait()
     loads[4].wait()
     query = dot(dst_mem.astype(bf16), w_query[...]) * (1.0 / 16.0)
-    query_hi, query_lo = split(query)
-    key_hi, key_lo = split(dot(table[...], w_key[:width, :]))
+    query_hi[...], query_lo[...] = split(query)
+    key_hi[...], key_lo[...] = split(dot(table[...], w_key[:width, :]))
     for h in range(HEADS):
         part = slice(h * 256, h * 256 + 256)
+        query_code[h] = dot(w_key[width:, part], query_hi[:, part], NT) + dot(
+            w_key[width:, part], query_lo[:, part], NT
+        )
         full[h] = (
             dot(key_hi[:, part], query_hi[:, part], NT)
             + dot(key_hi[:, part], query_lo[:, part], NT)
             + dot(key_lo[:, part], query_hi[:, part], NT)
         )
-        query_code[h] = dot(w_key[width:, part], query_hi[:, part], NT) + dot(
-            w_key[width:, part], query_lo[:, part], NT
-        )
-    val_hi, val_lo = split(dot(value_t[:, :width], table[...], NT))
+    loads[6].wait()
 
     def attend(piece, carry):
         lanes = pl.ds(pl.multiple_of(piece * 128, 128), 128)
+        value_hi[lanes, :width], value_lo[lanes, :] = split(
+            dot(value_t[lanes, :width], table[...], NT)
+        )
+        src_mem = dot(src_hot[lanes, :], table[...]).astype(bf16)
+        before[lanes, :] = dot(src_mem, w_msg1[:width, :]) + dot(
+            ev_code[lanes, :], w_msg1[2 * width :, :]
+        )
         near = ints[0:neigh, lanes]
         fine = [near[b * 8 : b * 8 + 8, :] & 7 for b in range(2)]
         coarse = [near[b * 8 : b * 8 + 8, :] >> 3 for b in range(2)]
 
+        zero = jnp.zeros((8, 128), f32)
+        def timed(i, sums):
+            sums = list(sums)
+            rows = pl.ds(pl.multiple_of(i * 8, 8), 8)
+            mine = [query_code[h, rows, lanes] for h in range(HEADS)]
+            for k in range(neigh):
+                one = code[k, rows, lanes]
+                for h in range(HEADS):
+                    sums[h * neigh + k] += one * mine[h]
+            return tuple(sums)
+
+        sums = lax.fori_loop(0, te // 8, timed, (zero,) * (HEADS * neigh), unroll=16)
         def look(i, found):
             found = list(found)
             for u in range(8):
@@ -320,20 +346,8 @@
                         found[h * 2 + b] = jnp.where(mask, taken, found[h * 2 + b])
             return tuple(found)
 
-        zero = jnp.zeros((8, 128), f32)
-        found = lax.fori_loop(0, 8, look, (zero,) * (2 * HEADS))
-
-        def timed(i, sums):
-            sums = list(sums)
-            rows = pl.ds(pl.multiple_of(i * 8, 8), 8)
-            mine = [query_code[h, rows, lanes] for h in range(HEADS)]
-            for k in range(neigh):
-                one = code[k, rows, lanes]
-                for h in range(HEADS):
-                    sums[h * neigh + k] += one * mine[h]
-            return tuple(sums)
-
-        sums = lax.fori_loop(0, te // 8, timed, (zero,) * (HEADS * neigh))
+        found = lax.fori_loop(0, 8, look, (zero,) * (2 * HEADS), unroll=8)
+
         whole = []
         weights = []
         for h in range(HEADS):
@@ -371,7 +385,7 @@
                     spread_lo[h, pl.ds(base, 16), lanes] = low
             return carry
 
-        lax.fori_loop(0, 8, put, 0)
+        lax.fori_loop(0, 8, put, 0, unroll=8)
         spread = [
             [jnp.broadcast_to(weights[h][k : k + 1, :], (8, 128)) for k in range(neigh)]
             for h in range(HEADS)
@@ -394,30 +408,24 @@
                 spread_lo[h, pl.ds(width + base, 16), lanes] = low
             return carry
 
-        lax.fori_loop(0, te // 16, mix, 0)
+        lax.fori_loop(0, te // 16, mix, 0, unroll=8)
         return carry
 
     lax.fori_loop(0, 4, attend, 0)
     att = []
     for h in range(HEADS):
         part = slice(h * 256, h * 256 + 256)
-        value = jnp.concatenate([val_hi[part], value_t[part, width:]], axis=1)
         att.append(
-            dot(value, spread_hi[h])
-            + dot(value, spread_lo[h])
-            + dot(val_lo[part], spread_hi[h, :width, :])
+            dot(value_hi[part, :], spread_hi[h])
+            + dot(value_hi[part, :], spread_lo[h])
+            + dot(value_lo[part, :], spread_hi[h, :width, :])
         )
     att = jnp.concatenate(att, axis=0).T.astype(bf16)
     loads[5].wait()
     emb[...] = (dst_mem + dot(att, w_out[...])).astype(bf16)
     emb_copy = pltpu.make_async_copy(emb, emb_hbm, emb_sem)
     emb_copy.start()
-    loads[6].wait()
-    hidden = (
-        dot(src_mem, w_msg1[:width, :])
-        + dot(emb[...], w_msg1[width : 2 * width, :])
-        + dot(ev_code[...], w_msg1[2 * width :, :])
-    )
+    hidden = before[...] + dot(emb[...], w_msg1[width : 2 * width, :])
     hidden = jnp.maximum(hidden, 0.0).astype(bf16)
     loads[7].wait()
     owns = []
@@ -489,12 +497,11 @@
     fresh,
     memory,
     moved,
+    emb,
     sem,
     in_sem,
     out_sem,
 ):
-    emb_copy = pltpu.make_async_copy(emb_hbm, emb_out, sem.at[0])
-    emb_copy.start()
     leader_copy = pltpu.make_async_copy(leader_hbm, leader, sem.at[1])
     leader_copy.start()
     fresh_copy = pltpu.make_async_copy(fresh_hbm, fresh, sem.at[2])
@@ -505,6 +512,8 @@
         block = pltpu.make_async_copy(memory_hbm.at[rows], memory.at[rows], in_sem.at[i])
         block.start()
         blocks.append(block)
+    emb_in = pltpu.make_async_copy(emb_hbm, emb, sem.at[0])
+    emb_in.start()
     leader_copy.wait()
     outs = []
     for i in range(8):
@@ -520,6 +529,10 @@
         out = pltpu.make_async_copy(moved.at[rows], new_hbm.at[rows], out_sem.at[i])
         out.start()
         outs.append(out)
+        if i == 3:
+            emb_in.wait()
+            emb_copy = pltpu.make_async_copy(emb, emb_out, sem.at[3])
+            emb_copy.start()
     emb_copy.wait()
     for out in outs:
         out.wait()
@@ -602,6 +615,10 @@
             sems,
             local(512, 512),
             local(512, 512, dtype=i32),
+            *[local(512, 512)] * 4,
+            local(512, 640),
+            local(512, 512),
+            local(512, 1024, dtype=f32),
         ],
         compiler_params=pltpu.CompilerParams(
             collective_id=0, has_side_effects=True, vmem_limit_bytes=60 << 20
@@ -632,7 +649,8 @@
             local(512, 512),
             local(*memory.shape),
             local(*memory.shape),
-            sems((3,)),
+            local(512, 512),
+            sems((4,)),
             sems((8,)),
             sems((8,)),
         ],

time: 77.4 us -> 63.9 us (0.83)
  Pallas kernels: 76.4 us -> 62.9 us
    pallas_call x1, Pallas kernels: 17.2 us -> 5.35 us  [per_device(): pl.pallas_call(place_kernel, out_shape=(jax.ShapeDtypeStruct(emb.shape, b...]
    pallas_call x1, Pallas kernels: 59.2 us -> 57.6 us  [per_device(): pl.pallas_call(window_kernel, out_shape=(jax.ShapeDtypeStruct((512, 512),...]
where the time goes in v4:
time: 63.9 us; the launch traced here: 63.7 us
  Pallas kernels  62.9 us (98%)
  between operations  0.81 us (1%)
    pallas_call x1, Pallas kernels, per_device(): pl.pallas_call(window_kernel, out_shape=(jax.ShapeDtypeStruct((512, 512),...  57.6 us
    pallas_call x1, Pallas kernels, per_device(): pl.pallas_call(place_kernel, out_shape=(jax.ShapeDtypeStruct(emb.shape, b...  5.35 us

profile of v4, /device:TPU:1, one launch (start us, length us, event | category | flops | bytes accessed | tf_op | source)
XLA Modules:
  0.0 63.7 jit_solution(17412019974353774847)
XLA Ops:
  0.6 57.6 %window.1 = (bf16[512,512]{1,0:T(8,128)(2,1)}, bf16[512,512]{1,0:T(8,128)(2,1)}, s32[8,512]{1,0:T(8,128)}) custom-call(s32[1,4,128]{2,1,0:T(4,128)} %bitcast.10, s32[1,512]{1,0:T(1,128)} %bitcast.11, s32[1,512]{1,0:T(1,128)} %bitcast.12, s32[1,512]{1,0:T(1,128)} %bitcast.13, s32[16,512]{1,0:T(8,128)} %bitcast.8, s32[1,512]{1,0:T(1,128)} %bitcast.14, ...), custom_call_target="tpu_custom_call" | custom-call | tf_op jit(solution)/shard_map/window/pallas_call | solution.py:568
  58.2 5.4 %place.1 = (bf16[512,512]{1,0:T(8,128)(2,1)}, bf16[2048,512]{1,0:T(8,128)(2,1)}) custom-call(s32[8,512]{1,0:T(8,128)} %get-tuple-element.5.leader_hbm, bf16[512,512]{1,0:T(8,128)(2,1)} %get-tuple-element.6.fresh_hbm, bf16[2048,512]{1,0:T(8,128)(2,1)} %memory_hbm.3, bf16[512,512]{1,0:T(8,128)(2,1)} %get-tuple-element.7.emb_hbm), custom_call_target="tpu_custom_call" | custom-call | tf_op jit(solution)/shard_map/place/pallas_call | solution.py:639

commit v5 on v4

--- a/solution.py
+++ b/solution.py
@@ -69,9 +69,7 @@
     w_msg1_hbm,
     w_msg2_hbm,
     w_input_hbm,
-    emb_hbm,
-    fresh_hbm,
-    lead_hbm,
+    joint_hbm,
     memory,
     w_hidden,
     w_query,
@@ -278,8 +276,10 @@
     earlier = match & (iota((512, 512), 0) < iota((512, 512), 1))
     earlier = jnp.sum(jnp.where(earlier, 1.0, 0.0), axis=0, keepdims=True)
     leader = jnp.where((earlier == 0.0) & (number_row > 0.0), asked_row, -1)
-    lead[...] = jnp.broadcast_to(leader, lead.shape)
-    lead_copy = pltpu.make_async_copy(lead, lead_hbm, lead_sem)
+    row = jnp.broadcast_to(leader + 64, lead.shape)
+    row = jnp.where(iota(lead.shape, 0) == 0, row >> 6, row & 63)
+    lead[...] = row.astype(f32).astype(bf16)
+    lead_copy = pltpu.make_async_copy(lead, joint_hbm.at[pl.ds(1024, 16)], lead_sem)
     lead_copy.start()
     ev_code[...] = cosine(cols[:, 2:3].astype(f32) * freq_row).astype(bf16)
     src_hot[...] = hot(iota((512, 512), 1) == cols[:, 0:1])
@@ -423,7 +423,7 @@
     att = jnp.concatenate(att, axis=0).T.astype(bf16)
     loads[5].wait()
     emb[...] = (dst_mem + dot(att, w_out[...])).astype(bf16)
-    emb_copy = pltpu.make_async_copy(emb, emb_hbm, emb_sem)
+    emb_copy = pltpu.make_async_copy(emb, joint_hbm.at[pl.ds(0, 512)], emb_sem)
     emb_copy.start()
     hidden = before[...] + dot(emb[...], w_msg1[width : 2 * width, :])
     hidden = jnp.maximum(hidden, 0.0).astype(bf16)
@@ -480,59 +480,28 @@
 
     lax.fori_loop(0, 8, update_rows, 0)
 
-    fresh_copy = pltpu.make_async_copy(fresh, fresh_hbm, new_sem)
+    fresh_copy = pltpu.make_async_copy(fresh, joint_hbm.at[pl.ds(512, 512)], new_sem)
     fresh_copy.start()
     lead_copy.wait()
     fresh_copy.wait()
 
 
-def place_kernel(
-    leader_hbm,
-    fresh_hbm,
-    memory_hbm,
-    emb_hbm,
-    emb_out,
-    new_hbm,
-    leader,
-    fresh,
-    memory,
-    moved,
-    emb,
-    sem,
-    in_sem,
-    out_sem,
-):
-    leader_copy = pltpu.make_async_copy(leader_hbm, leader, sem.at[1])
-    leader_copy.start()
-    fresh_copy = pltpu.make_async_copy(fresh_hbm, fresh, sem.at[2])
-    fresh_copy.start()
-    blocks = []
-    for i in range(8):
-        rows = pl.ds(i * 256, 256)
-        block = pltpu.make_async_copy(memory_hbm.at[rows], memory.at[rows], in_sem.at[i])
-        block.start()
-        blocks.append(block)
-    emb_in = pltpu.make_async_copy(emb_hbm, emb, sem.at[0])
-    emb_in.start()
-    leader_copy.wait()
+def place_kernel(joint, memory, emb_out, new_hbm, moved, emb_sem, out_sem):
+    emb_copy = pltpu.make_async_copy(joint.at[pl.ds(0, 512)], emb_out, emb_sem)
+    emb_copy.start()
+    row = joint[1024:1040, :].astype(f32)
+    leader = (row[0:1, :] * 64.0 + row[1:2, :] - 64.0).astype(i32)
     outs = []
     for i in range(8):
         rows = slice(i * 256, i * 256 + 256)
-        mask = iota((256, 512), 0) + i * 256 == leader[0:1, :]
+        mask = iota((256, 512), 0) + i * 256 == leader
         hit = jnp.max(jnp.where(mask, 1.0, 0.0), axis=1, keepdims=True)
-        if i == 0:
-            fresh_copy.wait()
-        new = dot(hot(mask), fresh[...])
-        blocks[i].wait()
+        new = dot(hot(mask), joint[512:1024, :])
         moved[rows, :] = jnp.where(hit > 0.0, new, memory[rows, :].astype(f32)).astype(bf16)
         rows = pl.ds(i * 256, 256)
         out = pltpu.make_async_copy(moved.at[rows], new_hbm.at[rows], out_sem.at[i])
         out.start()
         outs.append(out)
-        if i == 3:
-            emb_in.wait()
-            emb_copy = pltpu.make_async_copy(emb, emb_out, sem.at[3])
-            emb_copy.start()
     emb_copy.wait()
     for out in outs:
         out.wait()
@@ -565,15 +534,11 @@
         return pltpu.VMEM(shape, dtype)
 
     sems = pltpu.SemaphoreType.DMA
-    emb, fresh, leader = pl.pallas_call(
+    joint = pl.pallas_call(
         window_kernel,
-        out_shape=(
-            jax.ShapeDtypeStruct((512, 512), bf16),
-            jax.ShapeDtypeStruct((512, 512), bf16),
-            jax.ShapeDtypeStruct((8, 512), i32),
-        ),
+        out_shape=jax.ShapeDtypeStruct((1040, 512), bf16),
         in_specs=[vmem] * 8 + [anyw] * 9,
-        out_specs=(anyw,) * 3,
+        out_specs=anyw,
         scratch_shapes=[
             local(*memory.shape),
             *[local(*w.shape) for w in weights],
@@ -611,7 +576,7 @@
             local(512, 512),
             local(512, 512),
             local(512, 1536, dtype=f32),
-            local(8, 512, dtype=i32),
+            local(16, 512),
             sems,
             local(512, 512),
             local(512, 512, dtype=i32),
@@ -621,7 +586,7 @@
             local(512, 1024, dtype=f32),
         ],
         compiler_params=pltpu.CompilerParams(
-            collective_id=0, has_side_effects=True, vmem_limit_bytes=60 << 20
+            collective_id=0, has_side_effects=True, vmem_limit_bytes=58 << 20
         ),
         name="window",
     )(
@@ -639,24 +604,15 @@
     return pl.pallas_call(
         place_kernel,
         out_shape=(
-            jax.ShapeDtypeStruct(emb.shape, bf16),
+            jax.ShapeDtypeStruct((512, 512), bf16),
             jax.ShapeDtypeStruct(memory.shape, bf16),
         ),
-        in_specs=[anyw] * 4,
+        in_specs=[vmem, vmem],
         out_specs=(anyw, anyw),
-        scratch_shapes=[
-            local(8, 512, dtype=i32),
-            local(512, 512),
-            local(*memory.shape),
-            local(*memory.shape),
-            local(512, 512),
-            sems((4,)),
-            sems((8,)),
-            sems((8,)),
-        ],
-        compiler_params=pltpu.CompilerParams(vmem_limit_bytes=60 << 20),
+        scratch_shapes=[local(*memory.shape), sems, sems((8,))],
+        compiler_params=pltpu.CompilerParams(vmem_limit_bytes=12 << 20),
         name="place",
-    )(leader, fresh, memory, emb)
+    )(joint, memory)
 
 
 def solution(mesh):

time: 63.9 us -> 62.2 us (0.973)
  Pallas kernels: 62.9 us -> 59.9 us
  local copies, waits for them, and re-layouts: 0 us -> 1.23 us
    pallas_call x2, Pallas kernels: 62.9 us -> 59.9 us  [the longest x1 57.7 us: per_device(): pl.pallas_call(window_kernel, out_shape=jax.ShapeDtypeStruct((1040, 512),...]
    unnamed x0 -> x4, local copies, waits for them, and re-layouts: none -> 1.23 us
where the time goes in v5:
time: 62.2 us; the launch traced here: 62 us
  Pallas kernels  59.9 us (96%)
  local copies, waits for them, and re-layouts  1.23 us (2%)
  between operations  0.83 us (1%)
    pallas_call x1, Pallas kernels, per_device(): pl.pallas_call(window_kernel, out_shape=jax.ShapeDtypeStruct((1040, 512),...  57.7 us
    pallas_call x1, Pallas kernels, per_device(): pl.pallas_call(place_kernel, out_shape=(jax.ShapeDtypeStruct((512, 512),...  2.24 us

profile of v5, /device:TPU:1, one launch (start us, length us, event | category | flops | bytes accessed | tf_op | source)
XLA Modules:
  0.0 62.0 jit_solution(4551455390587506943)
XLA Ops:
  0.6 0.0 copy-start
  0.6 57.7 %window.1.joint = bf16[1040,512]{1,0:T(8,128)(2,1)} custom-call(s32[1,4,128]{2,1,0:T(4,128)} %bitcast.10, s32[1,512]{1,0:T(1,128)} %bitcast.11, s32[1,512]{1,0:T(1,128)} %bitcast.12, s32[1,512]{1,0:T(1,128)} %bitcast.13, s32[16,512]{1,0:T(8,128)} %bitcast.8, s32[1,512]{1,0:T(1,128)} %bitcast.14, s32[16,512]{1,0:T(8,128)} %bitcast.9, f32[1,128]{1,0:T(1,128)} %bitcast.15, ...), custom_call_target="tpu_custom_call" | custom-call | tf_op jit(solution)/shard_map/window/pallas_call | solution.py:537
  58.4 0.0 copy-done
  58.4 0.0 copy-start.1
  58.4 1.2 %copy-done.1 = bf16[1040,512]{1,0:T(8,128)(2,1)S(1)} copy-done((bf16[1040,512]{1,0:T(8,128)(2,1)S(1)}, bf16[1040,512]{1,0:T(8,128)(2,1)}, u32[]{:S(2)}) %copy-start.1) | copy-done | bytes 1064984
  59.6 2.2 %place.1 = (bf16[512,512]{1,0:T(8,128)(2,1)}, bf16[2048,512]{1,0:T(8,128)(2,1)}) custom-call(bf16[1040,512]{1,0:T(8,128)(2,1)S(1)} %copy-done.1, bf16[2048,512]{1,0:T(8,128)(2,1)S(1)} %copy-done), custom_call_target="tpu_custom_call" | custom-call | tf_op jit(solution)/shard_map/place/pallas_call | solution.py:604
Async XLA Ops:
  0.6 57.7 %copy-start = (bf16[2048,512]{1,0:T(8,128)(2,1)S(1)}, bf16[2048,512]{1,0:T(8,128)(2,1)}, u32[]{:S(2)}) copy-start(bf16[2048,512]{1,0:T(8,128)(2,1)} %memory.1) | copy-start | bytes 6291460
  58.4 1.2 %copy-start.1 = (bf16[1040,512]{1,0:T(8,128)(2,1)S(1)}, bf16[1040,512]{1,0:T(8,128)(2,1)}, u32[]{:S(2)}) copy-start(bf16[1040,512]{1,0:T(8,128)(2,1)} %window.1.joint) | copy-start | bytes 3194884

commit v6 on v5

--- a/solution.py
+++ b/solution.py
@@ -124,6 +124,7 @@
     value_hi,
     value_lo,
     before,
+    scale,
 ):
     groups, owners = 8, 16
     n = groups * owners
@@ -359,7 +360,8 @@
                 axis=0,
             ) + jnp.concatenate(found[h * 2 : h * 2 + 2], axis=0)
             score = jnp.exp(score - jnp.max(score, axis=0, keepdims=True))
-            weight = score / jnp.sum(score, axis=0, keepdims=True)
+            weight = score.astype(bf16).astype(f32)
+            scale[h : h + 1, lanes] = 1.0 / jnp.sum(weight, axis=0, keepdims=True)
             total = jnp.zeros((neigh, 128), f32)
             for k in range(neigh):
                 total += jnp.where(near == near[k : k + 1, :], weight[k : k + 1, :], 0.0)
@@ -380,9 +382,9 @@
                             jnp.where((which & 24) == 8, second, first)
                         )
                 for h in range(HEADS):
-                    high, low = split(jnp.concatenate(both[h], axis=0))
-                    spread_hi[h, pl.ds(base, 16), lanes] = high
-                    spread_lo[h, pl.ds(base, 16), lanes] = low
+                    spread_hi[h, pl.ds(base, 16), lanes] = jnp.concatenate(
+                        both[h], axis=0
+                    ).astype(bf16)
             return carry
 
         lax.fori_loop(0, 8, put, 0, unroll=8)
@@ -405,20 +407,23 @@
             for h in range(HEADS):
                 high, low = split(jnp.concatenate(both[h], axis=0))
                 spread_hi[h, pl.ds(width + base, 16), lanes] = high
-                spread_lo[h, pl.ds(width + base, 16), lanes] = low
+                spread_lo[h, pl.ds(base, 16), lanes] = low
             return carry
 
         lax.fori_loop(0, te // 16, mix, 0, unroll=8)
         return carry
 
-    lax.fori_loop(0, 4, attend, 0)
+    lax.fori_loop(0, 4, attend, 0, unroll=2)
     att = []
     for h in range(HEADS):
         part = slice(h * 256, h * 256 + 256)
         att.append(
-            dot(value_hi[part, :], spread_hi[h])
-            + dot(value_hi[part, :], spread_lo[h])
-            + dot(value_lo[part, :], spread_hi[h, :width, :])
+            (
+                dot(value_hi[part, :], spread_hi[h])
+                + dot(value_hi[part, width:], spread_lo[h])
+                + dot(value_lo[part, :], spread_hi[h, :width, :])
+            )
+            * scale[h : h + 1, :]
         )
     att = jnp.concatenate(att, axis=0).T.astype(bf16)
     loads[5].wait()
@@ -572,7 +577,7 @@
             local(2, 512, 512, dtype=f32),
             local(2, 128, 512, dtype=f32),
             local(2, 640, 512),
-            local(2, 640, 512),
+            local(2, 128, 512),
             local(512, 512),
             local(512, 512),
             local(512, 1536, dtype=f32),
@@ -584,6 +589,7 @@
             local(512, 640),
             local(512, 512),
             local(512, 1024, dtype=f32),
+            local(8, 512, dtype=f32),
         ],
         compiler_params=pltpu.CompilerParams(
             collective_id=0, has_side_effects=True, vmem_limit_bytes=58 << 20

time: 62.2 us -> 61.6 us (level)
  no operation moved by 1% of the time
where the time goes in v6:
time: 61.6 us; the launch traced here: 61.4 us
  Pallas kernels  59.3 us (96%)
  local copies, waits for them, and re-layouts  1.23 us (2%)
  between operations  0.83 us (1%)
    pallas_call x1, Pallas kernels, per_device(): pl.pallas_call(window_kernel, out_shape=jax.ShapeDtypeStruct((1040, 512),...  57.1 us
    pallas_call x1, Pallas kernels, per_device(): pl.pallas_call(place_kernel, out_shape=(jax.ShapeDtypeStruct((512, 512),...  2.24 us

profile of v6, /device:TPU:1, one launch (start us, length us, event | category | flops | bytes accessed | tf_op | source)
XLA Modules:
  0.0 61.4 jit_solution(7171817669436891967)
XLA Ops:
  0.6 0.0 copy-start
  0.6 57.1 %window.1.joint = bf16[1040,512]{1,0:T(8,128)(2,1)} custom-call(s32[1,4,128]{2,1,0:T(4,128)} %bitcast.10, s32[1,512]{1,0:T(1,128)} %bitcast.11, s32[1,512]{1,0:T(1,128)} %bitcast.12, s32[1,512]{1,0:T(1,128)} %bitcast.13, s32[16,512]{1,0:T(8,128)} %bitcast.8, s32[1,512]{1,0:T(1,128)} %bitcast.14, s32[16,512]{1,0:T(8,128)} %bitcast.9, f32[1,128]{1,0:T(1,128)} %bitcast.15, ...), custom_call_target="tpu_custom_call" | custom-call | tf_op jit(solution)/shard_map/window/pallas_call | solution.py:542
  57.7 0.0 copy-done
  57.8 0.0 copy-start.1
  57.8 1.2 %copy-done.1 = bf16[1040,512]{1,0:T(8,128)(2,1)S(1)} copy-done((bf16[1040,512]{1,0:T(8,128)(2,1)S(1)}, bf16[1040,512]{1,0:T(8,128)(2,1)}, u32[]{:S(2)}) %copy-start.1) | copy-done | bytes 1064984
  59.0 2.2 %place.1 = (bf16[512,512]{1,0:T(8,128)(2,1)}, bf16[2048,512]{1,0:T(8,128)(2,1)}) custom-call(bf16[1040,512]{1,0:T(8,128)(2,1)S(1)} %copy-done.1, bf16[2048,512]{1,0:T(8,128)(2,1)S(1)} %copy-done), custom_call_target="tpu_custom_call" | custom-call | tf_op jit(solution)/shard_map/place/pallas_call | solution.py:610
Async XLA Ops:
  0.6 57.1 %copy-start = (bf16[2048,512]{1,0:T(8,128)(2,1)S(1)}, bf16[2048,512]{1,0:T(8,128)(2,1)}, u32[]{:S(2)}) copy-start(bf16[2048,512]{1,0:T(8,128)(2,1)} %memory.1) | copy-start | bytes 6291460
  57.8 1.2 %copy-start.1 = (bf16[1040,512]{1,0:T(8,128)(2,1)S(1)}, bf16[1040,512]{1,0:T(8,128)(2,1)}, u32[]{:S(2)}) copy-start(bf16[1040,512]{1,0:T(8,128)(2,1)} %window.1.joint) | copy-start | bytes 3194884

commit v7 on v6

--- a/solution.py
+++ b/solution.py
@@ -249,11 +249,14 @@
     known_t = known.astype(f32).T.astype(i32)
 
     loads[0].wait()
+    asked_col = jnp.concatenate([known[:, s : s + 1] for s in range(4)], axis=0)
+    rows = dot(hot(iota((512, 2048), 1) == asked_col), memory[...])
+    picked[...] = rows.astype(bf16)
     for s in range(4):
-        rows = dot(hot(iota((n, 2048), 1) == known[:, s : s + 1]), memory[...])
-        picked[s * n : (s + 1) * n, :] = rows.astype(bf16)
         for c in range(4):
-            stage[pl.ds(s * 4 + c, n, stride=16), :] = rows[:, c * 128 : (c + 1) * 128]
+            stage[pl.ds(s * 4 + c, n, stride=16), :] = rows[
+                s * n : (s + 1) * n, c * 128 : (c + 1) * 128
+            ]
     outbox[...] = stage[...].astype(bf16).reshape(n, 16, 128)
 
     own = pltpu.make_async_copy(outbox.at[me], inbox.at[me], own_sem.at[2])
@@ -265,7 +268,6 @@
     loads[2].wait()
     value_t[...] = w_value[...].astype(f32).T.astype(bf16)
     value_hi[:, width:] = value_t[:, width:]
-    asked_col = jnp.concatenate([known[:, s : s + 1] for s in range(4)], axis=0)
     count_col = jnp.concatenate([known[:, s + 4 : s + 5] for s in range(4)], axis=0)
     asked_row = jnp.concatenate([known_t[s : s + 1, :] for s in range(4)], axis=1)
     count_row = jnp.concatenate([known_t[s + 4 : s + 5, :] for s in range(4)], axis=1)

time: 61.6 us -> 61.1 us (level)
  no operation moved by 1% of the time
where the time goes in v7:
time: 61.1 us; the launch traced here: 60.9 us
  Pallas kernels  58.8 us (96%)
  local copies, waits for them, and re-layouts  1.23 us (2%)
  between operations  0.83 us (1%)
    pallas_call x1, Pallas kernels, per_device(): pl.pallas_call(window_kernel, out_shape=jax.ShapeDtypeStruct((1040, 512),...  56.6 us
    pallas_call x1, Pallas kernels, per_device(): pl.pallas_call(place_kernel, out_shape=(jax.ShapeDtypeStruct((512, 512),...  2.24 us
    unnamed x4, local copies, waits for them, and re-layouts  1.23 us

profile of v7, /device:TPU:1, one launch (start us, length us, event | category | flops | bytes accessed | tf_op | source)
XLA Modules:
  0.0 60.9 jit_solution(6450028691973277583)
XLA Ops:
  0.6 0.0 copy-start
  0.6 56.6 %window.1.joint = bf16[1040,512]{1,0:T(8,128)(2,1)} custom-call(s32[1,4,128]{2,1,0:T(4,128)} %bitcast.10, s32[1,512]{1,0:T(1,128)} %bitcast.11, s32[1,512]{1,0:T(1,128)} %bitcast.12, s32[1,512]{1,0:T(1,128)} %bitcast.13, s32[16,512]{1,0:T(8,128)} %bitcast.8, s32[1,512]{1,0:T(1,128)} %bitcast.14, s32[16,512]{1,0:T(8,128)} %bitcast.9, f32[1,128]{1,0:T(1,128)} %bitcast.15, ...), custom_call_target="tpu_custom_call" | custom-call | tf_op jit(solution)/shard_map/window/pallas_call | solution.py:544
  57.3 0.0 copy-done
  57.3 0.0 copy-start.1
  57.3 1.2 %copy-done.1 = bf16[1040,512]{1,0:T(8,128)(2,1)S(1)} copy-done((bf16[1040,512]{1,0:T(8,128)(2,1)S(1)}, bf16[1040,512]{1,0:T(8,128)(2,1)}, u32[]{:S(2)}) %copy-start.1) | copy-done | bytes 1064984
  58.5 2.2 %place.1 = (bf16[512,512]{1,0:T(8,128)(2,1)}, bf16[2048,512]{1,0:T(8,128)(2,1)}) custom-call(bf16[1040,512]{1,0:T(8,128)(2,1)S(1)} %copy-done.1, bf16[2048,512]{1,0:T(8,128)(2,1)S(1)} %copy-done), custom_call_target="tpu_custom_call" | custom-call | tf_op jit(solution)/shard_map/place/pallas_call | solution.py:612
Async XLA Ops:
  0.6 56.6 %copy-start = (bf16[2048,512]{1,0:T(8,128)(2,1)S(1)}, bf16[2048,512]{1,0:T(8,128)(2,1)}, u32[]{:S(2)}) copy-start(bf16[2048,512]{1,0:T(8,128)(2,1)} %memory.1) | copy-start | bytes 6291460
  57.3 1.2 %copy-start.1 = (bf16[1040,512]{1,0:T(8,128)(2,1)S(1)}, bf16[1040,512]{1,0:T(8,128)(2,1)}, u32[]{:S(2)}) copy-start(bf16[1040,512]{1,0:T(8,128)(2,1)} %window.1.joint) | copy-start | bytes 3194884
